TPU v7x, 32 devices: a whole 2x2x4 slice. The times are simulated.
32 devices in a mesh: cfg: 2 (over core), seq: 4 (over z), blk: 4 (over y, x).
Axes of the slice: x: 2, y: 2, z: 4, core: 2. Of those that a mesh axis runs over, the one named last changes fastest.
Arguments:
- img_hidden: bfloat16 [2, 2, 2048, 1536], P('cfg', None, 'seq', 'blk'), may hold values from -15 to 15
- txt_hidden: bfloat16 [2, 2, 160, 1536], P('cfg', None, 'seq', 'blk'), may hold values from -6 to 6
- img_mod: float32 [2, 2, 6, 1536], P('cfg'), may hold values from -9 to 9
- txt_mod: float32 [2, 2, 2, 1536], P('cfg'), may hold values from -3 to 3
- out_mod: float32 [2, 2, 2, 1536], P('cfg'), may hold values from -3 to 3
- w_qkv: bfloat16 [3, 1536, 1536], P(None, None, 'blk'), may hold values from -0.25 to 0.25
- w_txt_kv: bfloat16 [2, 1536, 1536], P(None, None, 'blk'), may hold values from -0.25 to 0.25
- w_out: bfloat16 [1536, 1536], P('blk'), may hold values from -0.15625 to 0.15625
- w_fc1: bfloat16 [1536, 6144], P(None, 'blk'), may hold values from -0.15625 to 0.15625
- w_fc2: bfloat16 [6144, 1536], P('blk'), may hold values from -0.078125 to 0.078125
- w_proj: bfloat16 [1536, 64], P('blk'), may hold values from -0.15625 to 0.15625
- latent: float32 [2, 2048, 64], P(None, 'seq', 'cfg'), may hold values from -6 to 6
- lengths: int32 [2, 2], P('cfg'), may hold values from 1 to 154, as said below
- t_index: int32 [2], replicated, may hold values from 0 to 24
- stride: int32 [2], replicated, may hold values from 1 to 4
- guide: float32 [2], replicated, may hold values from 4 to 8
Outputs:
- new_latent: float32 [2, 2048, 64], P(None, 'seq', 'cfg')
- update_max: float32 [2], replicated
Inputs may be any that keep to these rules, and one draw needn't show every extreme that they name: `lengths`: at least one entry equals 154.
All inputs are finite; a program needn't handle non-finite values.
Results may differ from a plain program's by a relative error of at most 0.015.
Values may be sent and summed in bfloat16 or wider, within the bound.
A program may use at most 192 MiB of HBM per device.

v0:
```python
import jax
import jax.numpy as jnp
from jax import lax
from jax.sharding import PartitionSpec as P

HEAD = 64
STEPS = 28


EPSILON = 1e-06
BLOCK_ROWS = 512


def from_partner(value, axis, bit):
    return lax.ppermute(value, axis, [(i, i ^ 1 << bit) for i in range(lax.axis_size(axis))])


def normalize(values):
    values = values.astype(jnp.float32)
    center = jnp.mean(values, axis=-1, keepdims=True)
    spread = jnp.mean(jnp.square(values - center), axis=-1, keepdims=True)
    return (values - center) * lax.rsqrt(spread + EPSILON)


def modulate(values, scale_row, shift_row):
    return (normalize(values) * (1.0 + scale_row[:, None, :]) + shift_row[:, None, :]).astype(
        jnp.bfloat16
    )


def project(values, weight):
    flat_rows = values.reshape(-1, values.shape[-1])
    result = jnp.dot(flat_rows, weight, preferred_element_type=jnp.float32)
    return result.reshape(values.shape[:-1] + (weight.shape[-1],))


def noise_level(step_index):
    remain = 1.0 - step_index.astype(jnp.float32) / STEPS
    return 3.0 * remain / (1.0 + 2.0 * remain)


def own_columns(values, column_block, shard_width):
    return lax.dynamic_slice_in_dim(
        values, column_block * shard_width, shard_width, values.ndim - 1
    )


def per_device(
    img_hidden,
    txt_hidden,
    img_mod,
    txt_mod,
    out_mod,
    w_qkv,
    w_txt_kv,
    w_out,
    w_fc1,
    w_fc2,
    w_proj,
    latent,
    lengths,
    t_index,
    stride,
    guide,
):
    column_block = lax.axis_index("blk")
    shard_width = img_hidden.shape[3]
    model_width = shard_width * lax.axis_size("blk")
    image_full, text_full = (
        lax.all_gather(img_hidden[0], "blk", axis=2, tiled=True),
        lax.all_gather(txt_hidden[0], "blk", axis=2, tiled=True),
    )
    image_mod = img_mod[0]
    prompts = image_full.shape[0]
    img_rows = image_full.shape[1]
    attn_in = modulate(image_full, image_mod[:, 1], image_mod[:, 0])
    queries = project(attn_in, w_qkv[0]).astype(jnp.bfloat16)
    keys_img = project(attn_in, w_qkv[1]).astype(jnp.bfloat16)
    values_img = project(attn_in, w_qkv[2]).astype(jnp.bfloat16)
    text_norm = modulate(text_full, txt_mod[0][:, 0], txt_mod[0][:, 1])
    text_keys = project(text_norm, w_txt_kv[0]).astype(jnp.bfloat16)
    text_values = project(text_norm, w_txt_kv[1]).astype(jnp.bfloat16)
    head_width = queries.shape[2]
    head_count = head_width // HEAD
    query_heads = queries.reshape(prompts, img_rows, head_count, HEAD)
    text_limit = lengths[0]

    def attend_block(running_state, key_block, value_block, live_mask):
        accumulated, running, denominator = running_state
        key_count = key_block.shape[1]
        key_heads = key_block.reshape(prompts, key_count, head_count, HEAD)
        value_heads = value_block.reshape(prompts, key_count, head_count, HEAD)
        scores = jnp.einsum(
            "pqhe,pkhe->phqk", query_heads, key_heads, preferred_element_type=jnp.float32
        ) * HEAD ** (-0.5)
        if live_mask is not None:
            scores = jnp.where(live_mask[:, None, None, :], scores, -jnp.inf)
        updated = jnp.maximum(running, jnp.max(scores, axis=-1))
        factor = jnp.exp(running - updated)
        weights = jnp.exp(scores - updated[..., None])
        denominator = denominator * factor + jnp.sum(weights, axis=-1)
        mixed_values = jnp.einsum(
            "phqk,pkhe->phqe",
            weights.astype(jnp.bfloat16),
            value_heads,
            preferred_element_type=jnp.float32,
        )
        accumulated = accumulated * factor[..., None] + mixed_values
        return (accumulated, updated, denominator)

    initial = (
        jnp.zeros((prompts, head_count, img_rows, HEAD), jnp.float32),
        jnp.full((prompts, head_count, img_rows), -1e30, jnp.float32),
        jnp.zeros((prompts, head_count, img_rows), jnp.float32),
    )
    running_state = initial
    key_piece = lax.all_gather(keys_img, "seq", axis=1, tiled=True)
    value_piece = lax.all_gather(values_img, "seq", axis=1, tiled=True)
    key_count = key_piece.shape[1]
    blocks = key_count // BLOCK_ROWS
    key_split = key_piece.reshape(prompts, blocks, BLOCK_ROWS, head_width).transpose(1, 0, 2, 3)
    value_split = value_piece.reshape(prompts, blocks, BLOCK_ROWS, head_width).transpose(1, 0, 2, 3)

    def scan_step(state_now, operands):
        key_block, value_block = operands
        return (attend_block(state_now, key_block, value_block, None), None)

    running_state, unused = lax.scan(scan_step, running_state, (key_split, value_split))
    all_text_keys, all_text_values = (
        lax.all_gather(text_keys, "seq", axis=1, tiled=True),
        lax.all_gather(text_values, "seq", axis=1, tiled=True),
    )
    slot_index = jnp.arange(all_text_keys.shape[1], dtype=jnp.int32)
    text_mask = slot_index[None, :] < text_limit[:, None]
    accumulated, running, denominator = attend_block(
        running_state, all_text_keys, all_text_values, text_mask
    )
    attended = (accumulated / denominator[..., None]).astype(jnp.bfloat16)
    attended = attended.transpose(0, 2, 1, 3).reshape(prompts, img_rows, head_width)
    attn_part = project(attended, w_out)
    attn_sum = lax.psum(attn_part.astype(jnp.bfloat16), "blk").astype(jnp.float32)
    resid_full = (image_full.astype(jnp.float32) + image_mod[:, 2][:, None, :] * attn_sum).astype(
        jnp.bfloat16
    )
    resid_one = own_columns(resid_full, column_block, shard_width)
    mlp_in = modulate(resid_full, image_mod[:, 4], image_mod[:, 3])
    hidden_units = jax.nn.gelu(project(mlp_in, w_fc1), approximate=True).astype(jnp.bfloat16)
    mlp_sum = lax.psum_scatter(
        project(hidden_units, w_fc2).astype(jnp.bfloat16), "blk", scatter_dimension=2, tiled=True
    ).astype(jnp.float32)
    gate_mlp = own_columns(image_mod[:, 5], column_block, shard_width)
    resid_two = (resid_one.astype(jnp.float32) + gate_mlp[:, None, :] * mlp_sum).astype(
        jnp.bfloat16
    )
    stream = resid_two.astype(jnp.float32)
    row_sum, row_squares = lax.psum(
        (jnp.sum(stream, axis=-1), jnp.sum(stream * stream, axis=-1)), "blk"
    )
    center = row_sum / model_width
    spread = row_squares / model_width - center * center
    final_mod = out_mod[0]
    final_scale = own_columns(final_mod[:, 0], column_block, shard_width)
    final_shift = own_columns(final_mod[:, 1], column_block, shard_width)
    final_in = (
        (stream - center[..., None])
        * lax.rsqrt(spread[..., None] + EPSILON)
        * (1.0 + final_scale[:, None, :])
        + final_shift[:, None, :]
    ).astype(jnp.bfloat16)
    velocity_part = project(final_in, w_proj)
    half_index = lax.axis_index("cfg")
    channel_width = latent.shape[2]
    guide_scale = guide[:, None, None]
    velocity = lax.psum(velocity_part.astype(jnp.bfloat16), "blk").astype(jnp.float32)
    outgoing = own_columns(velocity, 1 - half_index, channel_width)
    other_half = from_partner(outgoing.astype(jnp.bfloat16), "cfg", 0).astype(outgoing.dtype)
    own_half = own_columns(velocity, half_index, channel_width)
    velocity_cond = jnp.where(half_index == 0, own_half, other_half)
    velocity_uncond = jnp.where(half_index == 0, other_half, own_half)
    guided = velocity_uncond + guide_scale * (velocity_cond - velocity_uncond)
    step_size = noise_level(t_index + stride) - noise_level(t_index)
    update = step_size[:, None, None] * guided
    new_latent = latent + update
    local_peak = jnp.max(jnp.abs(update), axis=(1, 2))
    peak_value = lax.pmax(local_peak, ("cfg", "seq"))
    return (new_latent, peak_value)


def solution(mesh):
    placed = (
        P("cfg", None, "seq", "blk"),
        P("cfg", None, "seq", "blk"),
        P("cfg", None, None, None),
        P("cfg", None, None, None),
        P("cfg", None, None, None),
        P(None, None, "blk"),
        P(None, None, "blk"),
        P("blk", None),
        P(None, "blk"),
        P("blk", None),
        P("blk", None),
        P(None, "seq", "cfg"),
        P("cfg", None),
        P(),
        P(),
        P(),
    )
    return jax.shard_map(
        per_device,
        mesh=mesh,
        in_specs=placed,
        out_specs=(P(None, "seq", "cfg"), P()),
        check_vma=False,
    )
```

profile of v0, /device:TPU:0, one launch (start us, length us, event | category | flops | bytes accessed | tf_op | source)
XLA Modules:
  0.0 552.0 jit_solution(2850391820597721948)
XLA Ops:
  8.0 0.9 copy.69
  9.6 46.8 %all-gather.10.cloned.1.call-done = bf16[1,2,512,1536]{3,2,1,0:T(8,128)(2,1)} async-done(((bf16[1,2,512,384]{3,2,1,0:T(8,128)(2,1)}), bf16[1,2,512,1536]{3,2,1,0:T(8,128)(2,1)}) %all-gather.10.cloned.1.call-update) | async-done | bytes 3145744 | tf_op jit(solution)/shard_map/all_gather | solution.py:70
  56.4 2.5 convert_reduce_fusion
  59.2 1.0 fusion.18
  60.2 4.0 convolution_convert_fusion.1
  64.4 5.0 convolution_convert_fusion.3
  69.5 9.2 %all-gather.1 = bf16[1,2,40,1536]{3,2,1,0:T(8,128)(2,1)S(1)} all-gather(bf16[1,2,40,384]{3,2,1,0:T(8,128)(2,1)S(1)} %copy-done.12), channel_id=3, replica_groups=mesh['cfg'=2,'seq'=4,'blk'=4] {'blk'}, dimensions={3}, use_global_device_ids=true | all-gather | bytes 307200 | tf_op jit(solution)/shard_map/all_gather | solution.py:71
  79.1 1.7 fusion.79
  80.8 16.4 %all_gather.22 = bf16[2,160,384]{2,1,0:T(8,128)(2,1)} all-gather(bf16[2,40,384]{2,1,0:T(8,128)(2,1)S(1)} %fusion.79), channel_id=1, replica_groups=mesh['cfg'=2,'seq'=4,'blk'=4] {'seq'}, dimensions={1}, use_global_device_ids=true | all-gather | bytes 307200 | tf_op jit(solution)/shard_map/all_gather | solution.py:130
  97.2 1.1 copy.39
  98.3 1.7 fusion.82
  100.0 16.7 %all_gather.23 = bf16[2,160,384]{2,1,0:T(8,128)(2,1)S(1)} all-gather(bf16[2,40,384]{2,1,0:T(8,128)(2,1)S(1)} %fusion.82), channel_id=1, replica_groups=mesh['cfg'=2,'seq'=4,'blk'=4] {'seq'}, dimensions={1}, use_global_device_ids=true | all-gather | bytes 307200 | tf_op jit(solution)/shard_map/all_gather | solution.py:131
  116.6 0.9 copy.40
  117.6 4.0 convolution_convert_fusion.2
  121.7 0.9 copy-done.2
  122.5 3.4 fusion.41
  125.9 9.6 %all-gather.8.cloned.1.call-done = bf16[2,2048,384]{2,1,0:T(8,128)(2,1)} async-done(((bf16[2,512,384]{2,1,0:T(8,128)(2,1)}), bf16[2,2048,384]{2,1,0:T(8,128)(2,1)}) %all-gather.8.cloned.1.call-update) | async-done | bytes 3145744 | tf_op jit(solution)/shard_map/all_gather | solution.py:118
  135.5 4.7 copy.38
  140.2 59.2 %all-gather.6.cloned.1.call-done = bf16[2,2048,384]{2,1,0:T(8,128)(2,1)} async-done(((bf16[2,512,384]{2,1,0:T(8,128)(2,1)}), bf16[2,2048,384]{2,1,0:T(8,128)(2,1)}) %all-gather.6.cloned.1.call-update) | async-done | bytes 3145744 | tf_op jit(solution)/shard_map/all_gather | solution.py:117
  199.4 4.7 copy.36
  204.1 87.5 %while.15 = (s32[]{:T(128)}, f32[2,6,512,64]{2,3,1,0:T(8,128)S(1)}, f32[2,6,512]{2,1,0:T(8,128)}, f32[2,6,512]{2,1,0:T(8,128)}, bf16[4,2,512,384]{2,3,1,0:T(8,12...) while((s32[]{:T(128)}, f32[2,6,512,64]{2,3,1,0:T(8,128)S(1)}, ...), condition=%wide.region_5.0_spmd.clone, body=%wide.region_2.5_spmd.clone.sunk | while | flops 831682560 | bytes 97419496 | solution.py:128
  204.1 1.5 constant_dynamic-slice_fusion.5
  205.5 8.1 %bitcast_reduce_fusion.2 = (f32[2,6,512]{2,1,0:T(8,128)}, f32[2,6,512,512]{3,2,1,0:T(8,128)}) fusion(bf16[2,512,6,64]{1,3,2,0:T(8,128)(2,1)S(1)} %bitcast.165, bf16[2,512,6,64]{1,3,2,0:T(8,128)(2,1)} %get-tuple-element.199), kind=kOutput, calls=%fused_computation.1.clone.1 | convolution fusion | flops 408938496 | bytes 14180352 | tf_op jit(solution)/shard_map/while/body/eval_jaxpr/pqhe,pkhe->phqk/dot_general | solution.py:93
  214.4 6.8 %fusion.134 = f32[2,6,512]{2,1,0:T(8,128)S(1)} fusion(f32[2,6,512,512]{3,2,1,0:T(8,128)} %get-tuple-element.172, f32[2,6,512]{2,1,0:T(8,128)S(1)} %select_maximum_fusion.2), kind=kLoop, calls=%fused_computation.3.clone.1 | loop fusion | flops 9431040 | bytes 12632064 | tf_op jit(solution)/shard_map/while/body/eval_jaxpr/reduce_sum | solution.py:101
  221.3 1.3 copy-done.1
  222.6 2.7 fusion.136
  225.9 1.5 constant_dynamic-slice_fusion.5
  227.4 8.1 %bitcast_reduce_fusion.2 = (f32[2,6,512]{2,1,0:T(8,128)}, f32[2,6,512,512]{3,2,1,0:T(8,128)}) fusion(bf16[2,512,6,64]{1,3,2,0:T(8,128)(2,1)S(1)} %bitcast.165, bf16[2,512,6,64]{1,3,2,0:T(8,128)(2,1)} %get-tuple-element.199), kind=kOutput, calls=%fused_computation.1.clone.1 | convolution fusion | flops 408938496 | bytes 14180352 | tf_op jit(solution)/shard_map/while/body/eval_jaxpr/pqhe,pkhe->phqk/dot_general | solution.py:93
  235.5 0.8 select_maximum_fusion.2
  236.3 6.8 %fusion.134 = f32[2,6,512]{2,1,0:T(8,128)S(1)} fusion(f32[2,6,512,512]{3,2,1,0:T(8,128)} %get-tuple-element.172, f32[2,6,512]{2,1,0:T(8,128)S(1)} %select_maximum_fusion.2), kind=kLoop, calls=%fused_computation.3.clone.1 | loop fusion | flops 9431040 | bytes 12632064 | tf_op jit(solution)/shard_map/while/body/eval_jaxpr/reduce_sum | solution.py:101
  243.2 1.3 copy-done.1
  244.5 2.7 fusion.136
  247.8 1.5 constant_dynamic-slice_fusion.5
  249.3 8.1 %bitcast_reduce_fusion.2 = (f32[2,6,512]{2,1,0:T(8,128)}, f32[2,6,512,512]{3,2,1,0:T(8,128)}) fusion(bf16[2,512,6,64]{1,3,2,0:T(8,128)(2,1)S(1)} %bitcast.165, bf16[2,512,6,64]{1,3,2,0:T(8,128)(2,1)} %get-tuple-element.199), kind=kOutput, calls=%fused_computation.1.clone.1 | convolution fusion | flops 408938496 | bytes 14180352 | tf_op jit(solution)/shard_map/while/body/eval_jaxpr/pqhe,pkhe->phqk/dot_general | solution.py:93
  257.4 0.8 select_maximum_fusion.2
  258.2 6.8 %fusion.134 = f32[2,6,512]{2,1,0:T(8,128)S(1)} fusion(f32[2,6,512,512]{3,2,1,0:T(8,128)} %get-tuple-element.172, f32[2,6,512]{2,1,0:T(8,128)S(1)} %select_maximum_fusion.2), kind=kLoop, calls=%fused_computation.3.clone.1 | loop fusion | flops 9431040 | bytes 12632064 | tf_op jit(solution)/shard_map/while/body/eval_jaxpr/reduce_sum | solution.py:101
  265.1 1.3 copy-done.1
  266.4 2.7 fusion.136
  269.7 1.5 constant_dynamic-slice_fusion.5
  271.2 8.1 %bitcast_reduce_fusion.2 = (f32[2,6,512]{2,1,0:T(8,128)}, f32[2,6,512,512]{3,2,1,0:T(8,128)}) fusion(bf16[2,512,6,64]{1,3,2,0:T(8,128)(2,1)S(1)} %bitcast.165, bf16[2,512,6,64]{1,3,2,0:T(8,128)(2,1)} %get-tuple-element.199), kind=kOutput, calls=%fused_computation.1.clone.1 | convolution fusion | flops 408938496 | bytes 14180352 | tf_op jit(solution)/shard_map/while/body/eval_jaxpr/pqhe,pkhe->phqk/dot_general | solution.py:93
  279.3 0.8 select_maximum_fusion.2
  280.1 6.8 %fusion.134 = f32[2,6,512]{2,1,0:T(8,128)S(1)} fusion(f32[2,6,512,512]{3,2,1,0:T(8,128)} %get-tuple-element.172, f32[2,6,512]{2,1,0:T(8,128)S(1)} %select_maximum_fusion.2), kind=kLoop, calls=%fused_computation.3.clone.1 | loop fusion | flops 9431040 | bytes 12632064 | tf_op jit(solution)/shard_map/while/body/eval_jaxpr/reduce_sum | solution.py:101
  287.0 1.3 copy-done.1
  288.3 2.7 fusion.136
  291.6 0.9 max.8
  292.5 3.4 fusion.47
  295.9 2.2 divide_convert_fusion
  298.1 3.5 convolution_convert_fusion
  301.8 85.9 %all-reduce.4.cloned.1.call-done = bf16[2,512,1536]{2,1,0:T(8,128)(2,1)} async-done(((bf16[2,512,1536]{2,1,0:T(8,128)(2,1)}), bf16[2,512,1536]{2,1,0:T(8,128)(2,1)}) %all-reduce.4.cloned.1.call-update) | async-done | bytes 3145744 | tf_op jit(solution)/shard_map/psum | solution.py:141
  387.7 4.0 convert_reduce_fusion.1
  391.8 1.6 copy-done.4
  393.4 1.0 fusion.22
  394.4 15.8 %fusion.38 = bf16[2,512,1536]{2,1,0:T(8,128)(2,1)} fusion(bf16[1536,1536]{1,0:T(8,128)(2,1)} %param.27, bf16[1536,1536]{1,0:T(8,128)(2,1)} %param.26, bf16[2,512,1536]{2,1,0:T(8,128)(2,1)} %copy-done.4, f32[2,1536]{1,0:T(2,128)S(1)} %get-tuple-element.113, f32[2,1536]{1,0:T(2,128)S(1)} %get-tuple-element.114, f32[2,512]{1,0:T(2,128)S(1)} %add_rsqrt_fusion.1, ...), kind=kOutput, calls=%fused_computation.50 | convolution fusion | flops 9688842240 | bytes 15761408 | tf_op jit(solution)/shard_map/dot_general | solution.py:33
  410.2 8.7 %copy.44 = bf16[2,512,1536]{1,0,2:T(2,128)(2,1)} copy(bf16[2,512,1536]{2,1,0:T(8,128)(2,1)} %fusion.38) | data formatting | bytes 6291456
  418.9 4.4 copy.57
  424.2 43.3 %reduce-scatter.4.cloned.1.call-done = bf16[384,1024]{1,0:T(8,128)(2,1)} async-done(((bf16[1536,1024]{1,0:T(8,128)(2,1)}), bf16[384,1024]{1,0:T(8,128)(2,1)}) %reduce-scatter.4.cloned.1.call-update) | async-done | bytes 786448
  467.4 2.6 reshape.158
  470.7 1.7 convert_reduce_fusion.2
  472.4 9.1 %all-reduce = (f32[2,512]{1,0:T(2,128)S(1)}, f32[2,512]{1,0:T(2,128)S(1)}) all-reduce(f32[2,512]{1,0:T(2,128)S(1)} %get-tuple-element.69, f32[2,512]{1,0:T(2,128)S(1)} %get-tuple-element.68), channel_id=1, replica_groups=mesh['cfg'=2,'seq'=4,'blk'=4] {'blk'}, use_global_device_ids=true, to_apply=%region_17.18 | all-reduce | flops 2048 | bytes 16384 | tf_op jit(solution)/shard_map/psum | solution.py:156
  481.5 1.2 convolution_convert_fusion.4
  482.7 42.1 %all-reduce.6.cloned.1.call-done = bf16[2,512,64]{1,2,0:T(8,128)(2,1)} async-done(((bf16[2,512,64]{1,2,0:T(8,128)(2,1)}), bf16[2,512,64]{1,2,0:T(8,128)(2,1)}) %all-reduce.6.cloned.1.call-update) | async-done | bytes 131088 | tf_op jit(solution)/shard_map/psum | solution.py:174
  524.8 0.9 convert_element_type.117
  525.9 1.2 collective-permute-done
  527.9 17.2 %pmax.7 = f32[2]{0:T(128)} all-reduce(f32[2]{0:T(128)S(1)} %get-tuple-element.97), channel_id=1, replica_groups=mesh['cfg'=2,'seq'=4,'blk'=4] {'cfg','seq'}, use_global_device_ids=true, to_apply=%region_20.21 | all-reduce | flops 2 | bytes 16 | tf_op jit(solution)/shard_map/pmax | solution.py:185
  (114 shorter events, 8.3 us)
Async XLA Ops:
  7.2 291.0 %copy-start = (bf16[384,1536]{1,0:T(8,128)(2,1)S(1)}, bf16[384,1536]{1,0:T(8,128)(2,1)}, u32[]{:S(2)}) copy-start(bf16[384,1536]{1,0:T(8,128)(2,1)} %param.25) | copy-start | bytes 3538948
  7.2 49.2 %all-gather.10.cloned.1.call-start = ((), (), s32[]{:S(2)}) async-start(), calls=%async_computation.5 | async-start | bytes 3932160 | tf_op jit(solution)/shard_map/all_gather | solution.py:70
  7.9 127.6 %all-gather.8.cloned.1.call-start = ((), (), s32[]{:S(2)}) async-start(), calls=%async_computation.2 | async-start | bytes 3932160 | tf_op jit(solution)/shard_map/all_gather | solution.py:118
  56.4 2.8 copy-start.3
  64.3 5.2 copy-start.12
  64.3 14.7 %copy-start.15 = (f32[1,2,2,1536]{3,2,1,0:T(2,128)S(1)}, f32[1,2,2,1536]{3,2,1,0:T(2,128)}, u32[]{:S(2)}) copy-start(f32[1,2,2,1536]{3,2,1,0:T(2,128)} %param.21) | copy-start | bytes 73732
  64.3 135.0 %all-gather.6.cloned.1.call-start = ((), (), s32[]{:S(2)}) async-start(), calls=%async_computation.1 | async-start | bytes 3932160 | tf_op jit(solution)/shard_map/all_gather | solution.py:117
  69.3 48.2 %copy-start.19 = (s32[1,2]{1,0:T(1,128)S(1)}, s32[1,2]{1,0:T(1,128)}, u32[]{:S(2)}) copy-start(s32[1,2]{1,0:T(1,128)} %param.30) | copy-start | bytes 28
  69.4 318.3 %all-reduce.4.cloned.1.call-start = ((), (), s32[]{:S(2)}) async-start(), calls=%async_computation.3 | async-start | bytes 6291456 | tf_op jit(solution)/shard_map/psum | solution.py:141
  121.7 0.9 copy-start.2
  214.4 6.9 %copy-start.6 = (f32[2,6,512]{2,1,0:T(8,128)S(1)}, f32[2,6,512]{2,1,0:T(8,128)}, u32[]{:S(2)}) copy-start(f32[2,6,512]{2,1,0:T(8,128)} %get-tuple-element.187) | copy-start | bytes 73732 | tf_op jit(solution)/shard_map/while
  214.4 6.9 %copy-start.8 = (f32[2,6,512]{2,1,0:T(8,128)S(1)}, f32[2,6,512]{2,1,0:T(8,128)}, u32[]{:S(2)}) copy-start(f32[2,6,512]{2,1,0:T(8,128)} %get-tuple-element.188) | copy-start | bytes 73732 | tf_op jit(solution)/shard_map/while
  214.4 8.2 %copy-start.1 = (f32[2,6,512,512]{3,2,1,0:T(8,128)S(1)}, f32[2,6,512,512]{3,2,1,0:T(8,128)}, u32[]{:S(2)}) copy-start(f32[2,6,512,512]{3,2,1,0:T(8,128)} %get-tuple-element.172) | copy-start | bytes 37748740 | tf_op jit(solution)/shard_map/while
  221.3 4.0 copy-start.9
  236.3 6.8 %copy-start.6 = (f32[2,6,512]{2,1,0:T(8,128)S(1)}, f32[2,6,512]{2,1,0:T(8,128)}, u32[]{:S(2)}) copy-start(f32[2,6,512]{2,1,0:T(8,128)} %get-tuple-element.187) | copy-start | bytes 73732 | tf_op jit(solution)/shard_map/while
  236.3 6.9 %copy-start.8 = (f32[2,6,512]{2,1,0:T(8,128)S(1)}, f32[2,6,512]{2,1,0:T(8,128)}, u32[]{:S(2)}) copy-start(f32[2,6,512]{2,1,0:T(8,128)} %get-tuple-element.188) | copy-start | bytes 73732 | tf_op jit(solution)/shard_map/while
  236.3 8.2 %copy-start.1 = (f32[2,6,512,512]{3,2,1,0:T(8,128)S(1)}, f32[2,6,512,512]{3,2,1,0:T(8,128)}, u32[]{:S(2)}) copy-start(f32[2,6,512,512]{3,2,1,0:T(8,128)} %get-tuple-element.172) | copy-start | bytes 37748740 | tf_op jit(solution)/shard_map/while
  243.2 4.0 copy-start.9
  258.2 6.8 %copy-start.6 = (f32[2,6,512]{2,1,0:T(8,128)S(1)}, f32[2,6,512]{2,1,0:T(8,128)}, u32[]{:S(2)}) copy-start(f32[2,6,512]{2,1,0:T(8,128)} %get-tuple-element.187) | copy-start | bytes 73732 | tf_op jit(solution)/shard_map/while
  258.2 6.9 %copy-start.8 = (f32[2,6,512]{2,1,0:T(8,128)S(1)}, f32[2,6,512]{2,1,0:T(8,128)}, u32[]{:S(2)}) copy-start(f32[2,6,512]{2,1,0:T(8,128)} %get-tuple-element.188) | copy-start | bytes 73732 | tf_op jit(solution)/shard_map/while
  258.2 8.2 %copy-start.1 = (f32[2,6,512,512]{3,2,1,0:T(8,128)S(1)}, f32[2,6,512,512]{3,2,1,0:T(8,128)}, u32[]{:S(2)}) copy-start(f32[2,6,512,512]{3,2,1,0:T(8,128)} %get-tuple-element.172) | copy-start | bytes 37748740 | tf_op jit(solution)/shard_map/while
  265.1 4.0 copy-start.9
  280.1 6.8 %copy-start.6 = (f32[2,6,512]{2,1,0:T(8,128)S(1)}, f32[2,6,512]{2,1,0:T(8,128)}, u32[]{:S(2)}) copy-start(f32[2,6,512]{2,1,0:T(8,128)} %get-tuple-element.187) | copy-start | bytes 73732 | tf_op jit(solution)/shard_map/while
  280.1 6.9 %copy-start.8 = (f32[2,6,512]{2,1,0:T(8,128)S(1)}, f32[2,6,512]{2,1,0:T(8,128)}, u32[]{:S(2)}) copy-start(f32[2,6,512]{2,1,0:T(8,128)} %get-tuple-element.188) | copy-start | bytes 73732 | tf_op jit(solution)/shard_map/while
  280.1 8.2 %copy-start.1 = (f32[2,6,512,512]{3,2,1,0:T(8,128)S(1)}, f32[2,6,512,512]{3,2,1,0:T(8,128)}, u32[]{:S(2)}) copy-start(f32[2,6,512,512]{3,2,1,0:T(8,128)} %get-tuple-element.172) | copy-start | bytes 37748740 | tf_op jit(solution)/shard_map/while
  287.0 4.0 copy-start.9
  291.6 4.3 copy-start.7
  291.6 4.3 copy-start.10
  291.6 4.3 copy-start.5
  298.1 3.6 copy-start.13
  298.1 3.6 copy-start.14
  301.7 165.8 %reduce-scatter.4.cloned.1.call-start = ((), (), s32[]{:S(2)}) async-start(), calls=%async_computation.6 | async-start | bytes 3932160
  391.7 1.7 copy-start.4
  418.9 5.2 copy-start.16
  423.3 58.2 %copy-start.18 = (bf16[384,64]{0,1:T(8,128)(2,1)S(1)}, bf16[384,64]{0,1:T(8,128)(2,1)}, u32[]{:S(2)}) copy-start(bf16[384,64]{0,1:T(8,128)(2,1)} %param.28) | copy-start | bytes 147460
  423.3 101.5 %all-reduce.6.cloned.1.call-start = ((), (), s32[]{:S(2)}) async-start(), calls=%async_computation.4 | async-start | bytes 262144 | tf_op jit(solution)/shard_map/psum | solution.py:174
  424.1 101.7 %copy-start.20 = (s32[2]{0:T(128)S(1)}, s32[2]{0:T(128)}, u32[]{:S(2)}) copy-start(s32[2]{0:T(128)} %param.31) | copy-start | bytes 28
  424.2 101.7 %copy-start.21 = (s32[2]{0:T(128)S(1)}, s32[2]{0:T(128)}, u32[]{:S(2)}) copy-start(s32[2]{0:T(128)} %param.32) | copy-start | bytes 28
  424.2 103.0 %copy-start.11 = (f32[2,512,32]{1,2,0:T(8,128)S(1)}, f32[2,512,32]{1,2,0:T(8,128)}, u32[]{:S(2)}) copy-start(f32[2,512,32]{1,2,0:T(8,128)} %param.29) | copy-start | bytes 393220
  424.2 102.9 %copy-start.17 = (f32[2]{0:T(128)S(1)}, f32[2]{0:T(128)}, u32[]{:S(2)}) copy-start(f32[2]{0:T(128)} %param.33) | copy-start | bytes 28
  525.8 1.3 collective-permute-start
Sparse Core Ops, SparseCore 0:
  9.8 46.5 all-gather.9
  64.4 71.0 all-gather.7
  137.1 62.2 all-gather.5
  301.8 85.8 all-reduce.3
  423.4 43.9 reduce-scatter.3
  482.9 41.9 all-reduce.5
where the time goes:
time: 553 us; the launch traced here: 552 us
  waiting for transfers between devices  289 us (52%)
  matrix products  85.7 us (15%)
  blocking collectives  68.6 us (12%)
  other arithmetic  47.8 us (9%)
  local copies, waits for them, and re-layouts  45.9 us (8%)
  between operations  14.5 us (3%)
    psum x1, waiting for transfers between devices, per_device(): lax.psum(attn_part.astype(jnp.bfloat16), 'blk').astype(jnp.float32)  85.9 us
    all_gather x1, waiting for transfers between devices, per_device(): key_piece = lax.all_gather(keys_img, 'seq', axis=1, tiled=True)  59.2 us
    all_gather x1, waiting for transfers between devices, per_device(): lax.all_gather(img_hidden[0], 'blk', axis=2, tiled=True)  46.8 us
    unnamed x7, waiting for transfers between devices  44 us
    psum x1, waiting for transfers between devices, per_device(): lax.psum(velocity_part.astype(jnp.bfloat16), 'blk').astype(jnp.float32)  42.1 us
    dot_general x8, matrix products, project(): result = jnp.dot(flat_rows, weight, preferred_element_type=jnp.float32)  37 us
    dot_general x5, matrix products, attend_block(): jnp.einsum('pqhe,pkhe->phqk', query_heads, key_heads, preferred_element_t...  35.9 us
    reduce_sum x5, other arithmetic, attend_block(): denominator = denominator * factor + jnp.sum(weights, axis=-1)  30.6 us
  transfers between devices with their start and end apart: 7, of which 7 were waited for; matrix products, arithmetic and copies ran while one was open for 5% of the time, Pallas kernels for 0%

commit v1 on v0

v1 whole, which is shorter than its diff:
```python
import functools

import jax
import jax.numpy as jnp
from jax import lax
from jax.experimental import pallas as pl
from jax.experimental.pallas import tpu as pltpu
from jax.sharding import PartitionSpec as P

HEAD = 64
STEPS = 28
EPSILON = 1e-06
PAIR = 2 * HEAD
Q_ROWS = 256
TEXT_PAD = 256


def normalize(values):
    values = values.astype(jnp.float32)
    center = jnp.mean(values, axis=-1, keepdims=True)
    spread = jnp.mean(jnp.square(values - center), axis=-1, keepdims=True)
    return (values - center) * lax.rsqrt(spread + EPSILON)


def modulate(values, scale_row, shift_row):
    return (normalize(values) * (1.0 + scale_row) + shift_row).astype(jnp.bfloat16)


def dot(a, b):
    return jnp.dot(a, b, preferred_element_type=jnp.float32)


def noise_level(step_index):
    remain = 1.0 - step_index.astype(jnp.float32) / STEPS
    return 3.0 * remain / (1.0 + 2.0 * remain)


def attend_kernel(first, last, *refs):
    refs = list(refs)
    q_ref, k_ref, v_ref = refs[:3]
    refs = refs[3:]
    if not first:
        acc_in, top_in = refs[:2]
        refs = refs[2:]
    if last:
        limit_ref, tk_ref, tv_ref = refs[:3]
        refs = refs[3:]
    q = q_ref[...]
    lane = lax.broadcasted_iota(jnp.int32, (1, PAIR), 1)
    scale = HEAD ** (-0.5)
    results = []
    for h in range(2):
        own = (lane < HEAD) if h == 0 else (lane >= HEAD)
        qh = jnp.where(own, q, jnp.zeros_like(q))
        pieces = [(k_ref[...], v_ref[...], None)]
        if last:
            slot = lax.broadcasted_iota(jnp.int32, (1, tk_ref.shape[0]), 1)
            pieces.append((tk_ref[...], tv_ref[...], slot < limit_ref[0]))
        scores = []
        top = None if first else top_in[h]
        for k, v, live in pieces:
            s = lax.dot_general(qh, k, (((1,), (1,)), ((), ())), preferred_element_type=jnp.float32)
            if live is not None:
                s = jnp.where(live, s, -jnp.inf)
            scores.append(s)
            peak = jnp.max(s, axis=-1, keepdims=True)
            if top is None:
                top = jnp.broadcast_to(peak, (q.shape[0], PAIR))
            else:
                top = jnp.maximum(top, peak)
        acc = None if first else acc_in[h] * jnp.exp((top_in[h] - top) * scale)
        for (k, v, live), s in zip(pieces, scores):
            p = jnp.exp((s - top[:, :1]) * scale).astype(jnp.bfloat16)
            vh = jnp.where(own, v, jnp.ones_like(v))
            part = dot(p, vh)
            acc = part if acc is None else acc + part
        results.append((acc, top))
    if last:
        (out_ref,) = refs
        outs = [acc / pltpu.roll(acc, HEAD, 1) for acc, _ in results]
        out_ref[...] = jnp.where(lane < HEAD, outs[0], outs[1]).astype(jnp.bfloat16)
    else:
        acc_out, top_out = refs
        for h in range(2):
            acc_out[h] = results[h][0]
            top_out[h] = results[h][1]


def attend_piece(queries, keys, values, state, text):
    rows, width = queries.shape
    count = keys.shape[0]
    pairs = width // PAIR
    first, last = state is None, text is not None
    q_spec = pl.BlockSpec((Q_ROWS, PAIR), lambda h, i: (i, h))
    kv_spec = pl.BlockSpec((count, PAIR), lambda h, i: (0, h))
    s_spec = pl.BlockSpec((2, Q_ROWS, PAIR), lambda h, i: (h, i, 0))
    args, specs = [queries, keys, values], [q_spec, kv_spec, kv_spec]
    if not first:
        args += list(state)
        specs += [s_spec, s_spec]
    if last:
        args += list(text)
        t_spec = pl.BlockSpec((text[1].shape[0], PAIR), lambda h, i: (0, h))
        specs += [pl.BlockSpec(memory_space=pltpu.SMEM), t_spec, t_spec]
        out_shape = jax.ShapeDtypeStruct((rows, width), jnp.bfloat16)
        out_specs = q_spec
    else:
        out_shape = [jax.ShapeDtypeStruct((2 * pairs, rows, PAIR), jnp.float32)] * 2
        out_specs = [s_spec, s_spec]
    return pl.pallas_call(
        functools.partial(attend_kernel, first, last),
        grid=(pairs, rows // Q_ROWS),
        in_specs=specs,
        out_specs=out_specs,
        out_shape=out_shape,
        compiler_params=pltpu.CompilerParams(vmem_limit_bytes=40 * 1024 * 1024),
        cost_estimate=pl.CostEstimate(
            flops=8 * rows * count * width,
            bytes_accessed=8 * rows * width,
            transcendentals=rows * count * width // HEAD,
        ),
    )(*args)


def per_device(
    img_hidden, txt_hidden, img_mod, txt_mod, out_mod, w_qkv, w_txt_kv, w_out,
    w_fc1, w_fc2, w_proj, latent, lengths, t_index, stride, guide,
):
    seq_size, blk_size = lax.axis_size("seq"), lax.axis_size("blk")
    group = seq_size // 2
    seq_at, blk_at, half = lax.axis_index("seq"), lax.axis_index("blk"), lax.axis_index("cfg")
    prompt = seq_at // group
    img_rows = img_hidden.shape[2]
    rows = 2 * img_rows
    own_rows = rows // blk_size

    def pick(values):
        return lax.dynamic_index_in_dim(values, prompt, 0, keepdims=False)

    def other(values):
        return lax.dynamic_index_in_dim(values, 1 - prompt, 0, keepdims=False)

    swap = [(i, (i + group) % seq_size) for i in range(seq_size)]
    swapped = lax.ppermute(other(img_hidden[0]), "seq", swap)
    mine = jnp.concatenate([pick(img_hidden[0]), swapped], axis=0)
    image = lax.all_gather(mine, "blk", axis=1, tiled=True)
    text = lax.all_gather(txt_hidden[0], "blk", axis=2, tiled=True)
    text = lax.all_gather(text, "seq", axis=1, tiled=True)
    text = pick(text)

    mod = pick(img_mod[0])
    tmod = pick(txt_mod[0])
    fmod = pick(out_mod[0])
    attn_in = modulate(image, mod[1:2], mod[0:1])
    keys = dot(attn_in, w_qkv[1]).astype(jnp.bfloat16)
    values = dot(attn_in, w_qkv[2]).astype(jnp.bfloat16)
    pieces = [(keys, values)]
    for k in range(1, group):
        turn = [
            (i, (i // group) * group + (i + k) % group) for i in range(seq_size)
        ]
        pieces.append((lax.ppermute(keys, "seq", turn), lax.ppermute(values, "seq", turn)))
    queries = dot(attn_in, w_qkv[0]).astype(jnp.bfloat16)
    text_norm = modulate(text, tmod[0:1], tmod[1:2])
    slots = text.shape[0]
    text_norm = jnp.pad(text_norm, ((0, -slots % TEXT_PAD), (0, 0)))
    text_keys = dot(text_norm, w_txt_kv[0]).astype(jnp.bfloat16)
    text_values = dot(text_norm, w_txt_kv[1]).astype(jnp.bfloat16)
    limit = pick(lengths[0])[None]

    full_out = lax.all_gather(w_out, "blk", axis=0, tiled=True)
    full_proj = lax.all_gather(w_proj, "blk", axis=0, tiled=True)

    state = None
    for at, (k, v) in enumerate(pieces):
        tail = (limit, text_keys, text_values) if at == len(pieces) - 1 else None
        state = attend_piece(queries, k, v, state, tail)
    attended = lax.all_gather(state, "blk", axis=1, tiled=True)
    resid_one = (image.astype(jnp.float32) + mod[2:3] * dot(attended, full_out)).astype(
        jnp.bfloat16
    )
    mlp_in = modulate(resid_one, mod[4:5], mod[3:4])
    hidden_units = jax.nn.gelu(dot(mlp_in, w_fc1), approximate=True).astype(jnp.bfloat16)
    mlp_sum = lax.psum_scatter(
        dot(hidden_units, w_fc2).astype(jnp.bfloat16), "blk", scatter_dimension=0, tiled=True
    ).astype(jnp.float32)
    resid_own = lax.dynamic_slice_in_dim(resid_one, blk_at * own_rows, own_rows, 0)
    resid_two = (resid_own.astype(jnp.float32) + mod[5:6] * mlp_sum).astype(jnp.bfloat16)
    final_in = modulate(resid_two, fmod[0:1], fmod[1:2])
    velocity = dot(final_in, full_proj).astype(jnp.bfloat16)

    velocity = lax.all_gather(velocity, "blk", axis=0, tiled=True)
    back = lax.ppermute(velocity[img_rows:], "seq", swap)
    here = velocity[:img_rows]
    both = jnp.where(prompt == 0, jnp.stack([here, back]), jnp.stack([back, here]))
    width = latent.shape[2]
    outgoing = lax.dynamic_slice_in_dim(both, (1 - half) * width, width, 2)
    own = lax.dynamic_slice_in_dim(both, half * width, width, 2).astype(jnp.float32)
    arrived = lax.ppermute(outgoing, "cfg", [(0, 1), (1, 0)]).astype(jnp.float32)
    cond = jnp.where(half == 0, own, arrived)
    uncond = jnp.where(half == 0, arrived, own)
    guided = uncond + guide[:, None, None] * (cond - uncond)
    step_size = noise_level(t_index + stride) - noise_level(t_index)
    update = step_size[:, None, None] * guided
    peak = lax.pmax(jnp.max(jnp.abs(update), axis=(1, 2)), ("cfg", "seq"))
    return (latent + update, peak)


def solution(mesh):
    placed = (
        P("cfg", None, "seq", "blk"),
        P("cfg", None, "seq", "blk"),
        P("cfg", None, None, None),
        P("cfg", None, None, None),
        P("cfg", None, None, None),
        P(None, None, "blk"),
        P(None, None, "blk"),
        P("blk", None),
        P(None, "blk"),
        P("blk", None),
        P("blk", None),
        P(None, "seq", "cfg"),
        P("cfg", None),
        P(),
        P(),
        P(),
    )
    return jax.shard_map(
        per_device,
        mesh=mesh,
        in_specs=placed,
        out_specs=(P(None, "seq", "cfg"), P()),
        check_vma=False,
    )
```

time: 553 us -> 302 us (0.55)
  waiting for transfers between devices: 289 us -> 125 us
  matrix products: 85.7 us -> 32.5 us
  local copies, waits for them, and re-layouts: 45.9 us -> 5.85 us
  Pallas kernels: 0 us -> 36.9 us
  other arithmetic: 47.8 us -> 10.9 us
  starting transfers between devices: 0.31 us -> 9.13 us
    psum x2 -> x0, waiting for transfers between devices: 128 us -> none  [the longest x1 85.9 us: per_device(): lax.psum(attn_part.astype(jnp.bfloat16), 'blk').astype(jnp.float32)]
    all_gather x3, waiting for transfers between devices: 116 us -> 53.6 us  [the longest x1 43.8 us: per_device(): attended = lax.all_gather(state, 'blk', axis=1, tiled=True)]
    dot_general x18 -> x8, matrix products: 85.7 us -> 32.5 us  [dot(): return jnp.dot(a, b, preferred_element_type=jnp.float32)]
    unnamed x7 -> x4, waiting for transfers between devices: 44 us -> 0.74 us
    pallas_call x0 -> x2, Pallas kernels: none -> 36.9 us  [attend_piece(): pl.pallas_call(functools.partial(attend_kernel, first, last), grid=(pairs...]
    ppermute x1 -> x5, waiting for transfers between devices: 1.2 us -> 36.4 us  [the longest x1 17.5 us: per_device(): swapped = lax.ppermute(other(img_hidden[0]), 'seq', swap)]
    reduce_scatter x0 -> x1, waiting for transfers between devices: none -> 33.9 us  [per_device(): lax.psum_scatter(dot(hidden_units, w_fc2).astype(jnp.bfloat16), 'blk', sc...]
    reduce_sum x6 -> x0, other arithmetic: 32.3 us -> none  [the longest x5 30.6 us: attend_block(): denominator = denominator * factor + jnp.sum(weights, axis=-1)]
  transfers between devices with their start and end apart: 7 -> 9, of which waited for: 7 -> 7; matrix products, arithmetic and copies ran while one was open for 5% -> 5% of each run, Pallas kernels for 0% -> 12%
where the time goes in v1:
time: 302 us
  waiting for transfers between devices  125 us (41%)
  blocking collectives  67.8 us (22%)
  Pallas kernels  36.9 us (12%)
  matrix products  32.5 us (11%)
  between operations  14.1 us (5%)
  other arithmetic  10.9 us (4%)
  starting transfers between devices  9.13 us (3%)
  local copies, waits for them, and re-layouts  5.85 us (2%)
    all_gather x1, waiting for transfers between devices, per_device(): attended = lax.all_gather(state, 'blk', axis=1, tiled=True)  43.8 us
    pallas_call x2, Pallas kernels, attend_piece(): pl.pallas_call(functools.partial(attend_kernel, first, last), grid=(pairs...  36.9 us
    reduce_scatter x1, waiting for transfers between devices, per_device(): lax.psum_scatter(dot(hidden_units, w_fc2).astype(jnp.bfloat16), 'blk', sc...  33.9 us
    dot_general x8, matrix products, dot(): return jnp.dot(a, b, preferred_element_type=jnp.float32)  32.5 us
    all_gather x1, blocking collectives, per_device(): text = lax.all_gather(text, 'seq', axis=1, tiled=True)  21.6 us
    pmax x1, blocking collectives, per_device(): peak = lax.pmax(jnp.max(jnp.abs(update), axis=(1, 2)), ('cfg', 'seq'))  17.9 us
    ppermute x1, waiting for transfers between devices, per_device(): swapped = lax.ppermute(other(img_hidden[0]), 'seq', swap)  17.5 us
    ppermute x1, waiting for transfers between devices, per_device(): lax.ppermute(values, 'seq', turn)  14.9 us
  transfers between devices with their start and end apart: 9, of which 7 were waited for; matrix products, arithmetic and copies ran while one was open for 5% of the time, Pallas kernels for 12%

profile of v1, /device:TPU:0, one launch (start us, length us, event | category | flops | bytes accessed | tf_op | source)
XLA Modules:
  0.0 301.8 jit_solution(3001268244334517725)
XLA Ops:
  7.2 0.0 copy-start
  7.2 0.0 copy-start.9
  7.2 0.0 copy-start.8
  7.2 0.0 all-gather.6.cloned.1.call-start
  7.3 1.2 dynamic-slice_bitcast_fusion.1
  8.5 4.1 %collective-permute-start = (bf16[512,384]{1,0:T(8,128)(2,1)S(1)}, bf16[512,384]{1,0:T(8,128)(2,1)S(1)}, u32[]{:S(2)}, u32[]{:S(2)}) collective-permute-start(bf16[512,384]{1,0:T(8,128)(2,1)S(1)} %get-tuple-element.19), channel_id=1, source_target_pairs={{0,8},{4,12},{8,0},{12,4},{1,9},{5,13},{9,1},{13,5},{2,10},{6,14},... | collective-permute-start | bytes 1179656 | tf_op jit(solution)/shard_map/ppermute | solution.py:144
  12.6 17.5 %collective-permute-done = bf16[512,384]{1,0:T(8,128)(2,1)S(1)} collective-permute-done((bf16[512,384]{1,0:T(8,128)(2,1)S(1)}, bf16[512,384]{1,0:T(8,128)(2,1)S(1)}, u32[]{:S(2)}, u32[]{:S(2)}) %collective-permute-start) | collective-permute-done | bytes 393248 | tf_op jit(solution)/shard_map/ppermute | solution.py:144
  30.1 1.0 pad_maximum_fusion
  31.1 0.0 all-gather.6.cloned.1.call-update
  31.2 0.0 all-gather.10.cloned.1.call-start
  31.2 0.7 all-gather.10.cloned.1.call-update
  31.9 0.0 all-gather.8.cloned.1.call-start
  32.0 0.1 fusion.82
  32.2 9.3 %all-gather = bf16[1,2,40,1536]{3,2,1,0:T(8,128)(2,1)S(1)} all-gather(bf16[1,2,40,384]{3,2,1,0:T(8,128)(2,1)S(1)} %copy-done.6), channel_id=2, replica_groups=mesh['cfg'=2,'seq'=4,'blk'=4] {'blk'}, dimensions={3}, use_global_device_ids=true | all-gather | bytes 307200 | tf_op jit(solution)/shard_map/all_gather | solution.py:147
  41.5 21.6 %all-gather.1 = bf16[1,2,160,1536]{3,2,1,0:T(8,128)(2,1)S(1)} all-gather(bf16[1,2,40,1536]{3,2,1,0:T(8,128)(2,1)S(1)} %all-gather), channel_id=3, replica_groups=mesh['cfg'=2,'seq'=4,'blk'=4] {'seq'}, dimensions={2}, use_global_device_ids=true | all-gather | bytes 1228800 | tf_op jit(solution)/shard_map/all_gather | solution.py:148
  63.1 0.1 convert_reduce_fusion.3
  63.2 0.3 fusion.63
  63.5 0.4 fusion.66
  63.9 0.8 copy-done.3
  64.7 1.8 fusion.54.refs_6_
  66.5 9.8 %all-gather.6.cloned.1.call-done = bf16[1024,1536]{1,0:T(8,128)(2,1)} async-done(((bf16[1024,384]{1,0:T(8,128)(2,1)}), bf16[1024,1536]{1,0:T(8,128)(2,1)}) %all-gather.6.cloned.1.call-update) | async-done | bytes 3145744 | tf_op jit(solution)/shard_map/all_gather | solution.py:146
  76.4 2.5 convert_reduce_fusion
  78.9 0.3 copy-done.1
  79.2 1.0 fusion.4
  80.2 1.5 fusion.7
  81.7 0.5 copy-done.12
  82.2 1.8 convolution_convert_fusion.2.refs_1_
  84.0 0.0 copy-start.13
  84.0 1.6 collective-permute-start.1
  85.5 1.8 convolution_convert_fusion.1.refs_2_
  87.3 0.6 collective-permute-start.2
  87.9 0.0 copy-done.4
  87.9 0.6 fusion.57.refs_7_
  88.5 0.0 copy-done
  88.5 0.6 constant_dynamic-slice_fusion.1
  89.1 1.8 convolution_convert_fusion.3.refs_0_
  90.9 14.4 %shard_map.167 = (f32[6,1024,128]{2,1,0:T(8,128)S(1)}, f32[6,1024,128]{2,1,0:T(8,128)S(1)}) custom-call(bf16[1024,384]{1,0:T(8,128)(2,1)S(1)} %convolution_convert_fusion.3.refs_0_, bf16[1024,384]{1,0:T(8,128)(2,1)S(1)} %convolution_convert_fusion.2.refs_1_, bf16[1024,384]{1,0:T(8,128)(2,1)S(1)} %convolution_convert_fusion.1.refs_2_), custom_call_target="tpu_custom_call" | custom-call | flops 3221225472 | bytes 3145728 | tf_op jit(solution)/shard_map/pallas_call | solution.py:110
  105.3 0.0 collective-permute-done.1.refs_1_
  105.3 14.9 %collective-permute-done.2.refs_2_ = bf16[1024,384]{1,0:T(8,128)(2,1)S(1)} collective-permute-done((bf16[1024,384]{1,0:T(8,128)(2,1)S(1)}, bf16[1024,384]{1,0:T(8,128)(2,1)S(1)}, u32[]{:S(2)}, u32[]{:S(2)}) %collective-permute-start.2) | collective-permute-done | bytes 786464 | tf_op jit(solution)/shard_map/ppermute | solution.py:162
  120.2 22.5 %shard_map.168 = bf16[1024,384]{1,0:T(8,128)(2,1)} custom-call(bf16[1024,384]{1,0:T(8,128)(2,1)S(1)} %convolution_convert_fusion.3.refs_0_, bf16[1024,384]{1,0:T(8,128)(2,1)S(1)} %collective-permute-done.1.refs_1_, bf16[1024,384]{1,0:T(8,128)(2,1)S(1)} %collective-permute-done.2.refs_2_, f32[6,1024,128]{2,1,0:T(8,128)S(1)} %get-tuple-element.4.refs_3_, ...), custom_call_target="tpu_custom_call" | custom-call | flops 3221225472 | bytes 3145728 | tf_op jit(solution)/shard_map/pallas_call | solution.py:110
  142.7 0.0 all-gather.8.cloned.1.call-update
  142.7 0.2 reduce-scatter.2.cloned.1.call-start
  142.9 0.0 all-gather.10.cloned.1.call-done
  142.9 43.8 %all-gather.8.cloned.1.call-done = bf16[1024,1536]{1,0:T(8,128)(2,1)} async-done(((bf16[1024,384]{1,0:T(8,128)(2,1)}), bf16[1024,1536]{1,0:T(8,128)(2,1)}) %all-gather.8.cloned.1.call-update) | async-done | bytes 3145744 | tf_op jit(solution)/shard_map/all_gather | solution.py:178
  186.7 8.3 %convert_reduce_fusion.1 = (f32[1024]{0:T(1024)S(1)}, bf16[1024,1536]{1,0:T(8,128)(2,1)S(1)}) fusion(bf16[1024,1536]{1,0:T(8,128)(2,1)} %all-gather.8.cloned.1.call-done, bf16[1536,1536]{1,0:T(8,128)(2,1)} %all-gather.10.cloned.1.call-done, f32[1536]{0:T(1024)S(1)} %get-tuple-element.10, bf16[1024,1536]{1,0:T(8,128)(2,1)S(1)} %copy-done.1), kind=kOutput, calls=%fused_computation.5 | convolution fusion | flops 4841274368 | bytes 14166016 | tf_op jit(solution)/shard_map/dot_general | solution.py:30
  195.1 1.6 copy-done.2
  196.7 1.0 fusion.8
  197.7 15.9 %convolution_convert_fusion = bf16[1024,1536]{1,0:T(8,128)(2,1)} fusion(bf16[1536,1536]{1,0:T(8,128)(2,1)} %param.25, bf16[1536,1536]{1,0:T(8,128)(2,1)} %param.24, bf16[1024,1536]{1,0:T(8,128)(2,1)} %copy-done.2, f32[1536]{0:T(1024)S(1)} %get-tuple-element.11, f32[1536]{0:T(1024)S(1)} %get-tuple-element.7, f32[1024]{0:T(1024)S(1)} %add_rsqrt_fusion, ...), kind=kOutput, calls=%fused_computation.27 | convolution fusion | flops 9688842240 | bytes 15749120 | tf_op jit(solution)/shard_map/dot_general | solution.py:30
  213.6 0.0 reduce-scatter.2.cloned.1.call-update
  213.6 0.7 copy-done.10
  214.4 0.0 copy-done.7
  214.4 10.1 %all_gather.26 = bf16[1536,64]{0,1:T(8,128)(2,1)S(1)} all-gather(bf16[384,64]{0,1:T(8,128)(2,1)S(1)} %copy-done.7), channel_id=1, replica_groups=mesh['cfg'=2,'seq'=4,'blk'=4] {'blk'}, dimensions={0}, use_global_device_ids=true | all-gather | bytes 245760 | tf_op jit(solution)/shard_map/all_gather | solution.py:172
  224.6 33.9 %reduce-scatter.2.cloned.1.call-done = bf16[256,1536]{1,0:T(8,128)(2,1)} async-done(((bf16[1024,1536]{1,0:T(8,128)(2,1)}), bf16[256,1536]{1,0:T(8,128)(2,1)}) %reduce-scatter.2.cloned.1.call-update) | async-done | bytes 786448 | tf_op jit(solution)/shard_map/reduce_scatter | solution.py:184
  258.4 1.8 convert_reduce_fusion.2
  260.2 0.4 fusion.34
  260.6 0.5 convolution_convert_fusion.4
  261.1 8.9 %all_gather.27 = bf16[1024,64]{0,1:T(8,128)(2,1)S(1)} all-gather(bf16[256,64]{0,1:T(8,128)(2,1)S(1)} %convolution_convert_fusion.4), channel_id=1, replica_groups=mesh['cfg'=2,'seq'=4,'blk'=4] {'blk'}, dimensions={0}, use_global_device_ids=true | all-gather | bytes 163840 | tf_op jit(solution)/shard_map/all_gather | solution.py:192
  270.0 2.5 collective-permute-start.3
  272.5 2.8 collective-permute-done.3
  275.3 0.1 collective-permute-start.4
  275.4 1.2 collective-permute-done.4
  276.6 0.0 copy-done.11
  276.6 0.8 abs_reduce_fusion
  277.4 17.9 %pmax.7 = f32[2]{0:T(128)} all-reduce(f32[2]{0:T(128)S(1)} %get-tuple-element.20), channel_id=1, replica_groups=mesh['cfg'=2,'seq'=4,'blk'=4] {'cfg','seq'}, use_global_device_ids=true, to_apply=%region_10.11 | all-reduce | flops 2 | bytes 16 | tf_op jit(solution)/shard_map/pmax | solution.py:205
  (33 shorter events, 0.2 us)
Async XLA Ops:
  7.2 81.3 %copy-start = (s32[1,2]{1,0:T(1,128)S(1)}, s32[1,2]{1,0:T(1,128)}, u32[]{:S(2)}) copy-start(s32[1,2]{1,0:T(1,128)} %param.28) | copy-start | bytes 28
  7.2 24.8 %copy-start.9 = (f32[1,2,2,1536]{3,2,1,0:T(2,128)S(1)}, f32[1,2,2,1536]{3,2,1,0:T(2,128)}, u32[]{:S(2)}) copy-start(f32[1,2,2,1536]{3,2,1,0:T(2,128)} %param.19) | copy-start | bytes 73732
  7.2 24.8 %copy-start.8 = (f32[1,2,6,1536]{3,1,2,0:T(2,128)S(1)}, f32[1,2,6,1536]{3,1,2,0:T(2,128)}, u32[]{:S(2)}) copy-start(f32[1,2,6,1536]{3,1,2,0:T(2,128)} %param.18) | copy-start | bytes 221188
  7.2 25.0 %copy-start.6 = (bf16[1,2,40,384]{3,2,1,0:T(8,128)(2,1)S(1)}, bf16[1,2,40,384]{3,2,1,0:T(8,128)(2,1)}, u32[]{:S(2)}) copy-start(bf16[1,2,40,384]{3,2,1,0:T(8,128)(2,1)} %param.17) | copy-start | bytes 184324
  7.2 69.1 %all-gather.6.cloned.1.call-start = ((), (), s32[]{:S(2)}) async-start(), calls=%async_computation.1 | async-start | bytes 3932160 | tf_op jit(solution)/shard_map/all_gather | solution.py:146
  8.5 21.6 %collective-permute-start = (bf16[512,384]{1,0:T(8,128)(2,1)S(1)}, bf16[512,384]{1,0:T(8,128)(2,1)S(1)}, u32[]{:S(2)}, u32[]{:S(2)}) collective-permute-start(bf16[512,384]{1,0:T(8,128)(2,1)S(1)} %get-tuple-element.19), channel_id=1, source_target_pairs={{0,8},{4,12},{8,0},{12,4},{1,9},{5,13},{9,1},{13,5},{2,10},{6,14},... | collective-permute-start | bytes 1179656 | tf_op jit(solution)/shard_map/ppermute | solution.py:144
  31.2 111.8 %all-gather.10.cloned.1.call-start = ((), (), s32[]{:S(2)}) async-start(), calls=%async_computation.3 | async-start | bytes 5898240 | tf_op jit(solution)/shard_map/all_gather | solution.py:171
  31.9 154.8 %all-gather.8.cloned.1.call-start = ((), (), s32[]{:S(2)}) async-start(), calls=%async_computation.2 | async-start | bytes 3932160 | tf_op jit(solution)/shard_map/all_gather | solution.py:178
  63.9 0.8 copy-start.3
  76.3 2.8 copy-start.1
  80.2 2.0 copy-start.12
  84.0 4.0 %copy-start.4 = (bf16[160,1536]{1,0:T(8,128)(2,1)S(1)}, bf16[160,1536]{1,0:T(8,128)(2,1)}, u32[]{:S(2)}) copy-start(bf16[160,1536]{1,0:T(8,128)(2,1)} %copy-done.3) | copy-start | bytes 1474564
  84.0 4.0 %copy-start.13 = (bf16[2,1536,384]{2,1,0:T(8,128)(2,1)S(1)}, bf16[2,1536,384]{2,1,0:T(8,128)(2,1)}, u32[]{:S(2)}) copy-start(bf16[2,1536,384]{2,1,0:T(8,128)(2,1)} %param.22) | copy-start | bytes 7077892
  84.0 21.3 %collective-permute-start.1 = (bf16[1024,384]{1,0:T(8,128)(2,1)S(1)}, bf16[1024,384]{1,0:T(8,128)(2,1)S(1)}, u32[]{:S(2)}, u32[]{:S(2)}) collective-permute-start(bf16[1024,384]{1,0:T(8,128)(2,1)S(1)} %convolution_convert_fusion.2.refs_1_), channel_id=1, source_target_pairs={{0,4},{4,0},{8,12},{12,8},{1,5},{5,1},{9,13},{13,9},{2,6},{6,2},{1... | collective-permute-start | bytes 2359304 | tf_op jit(solution)/shard_map/ppermute | solution.py:162
  87.3 32.9 %collective-permute-start.2 = (bf16[1024,384]{1,0:T(8,128)(2,1)S(1)}, bf16[1024,384]{1,0:T(8,128)(2,1)S(1)}, u32[]{:S(2)}, u32[]{:S(2)}) collective-permute-start(bf16[1024,384]{1,0:T(8,128)(2,1)S(1)} %convolution_convert_fusion.1.refs_2_), channel_id=1, source_target_pairs={{0,4},{4,0},{8,12},{12,8},{1,5},{5,1},{9,13},{13,9},{2,6},{6,2},{1... | collective-permute-start | bytes 2359304 | tf_op jit(solution)/shard_map/ppermute | solution.py:162
  142.7 115.7 %reduce-scatter.2.cloned.1.call-start = ((), (), s32[]{:S(2)}) async-start(), calls=%async_computation.4 | async-start | bytes 3932160 | tf_op jit(solution)/shard_map/reduce_scatter | solution.py:184
  195.0 1.7 copy-start.2
  213.6 0.7 copy-start.10
  213.6 0.8 copy-start.7
  258.4 16.9 %copy-start.14 = (s32[2]{0:T(128)S(1)}, s32[2]{0:T(128)}, u32[]{:S(2)}) copy-start(s32[2]{0:T(128)} %param.29) | copy-start | bytes 28
  258.4 16.9 %copy-start.15 = (s32[2]{0:T(128)S(1)}, s32[2]{0:T(128)}, u32[]{:S(2)}) copy-start(s32[2]{0:T(128)} %param.30) | copy-start | bytes 28
  258.4 18.2 %copy-start.5 = (f32[2,512,32]{1,2,0:T(8,128)S(1)}, f32[2,512,32]{1,2,0:T(8,128)}, u32[]{:S(2)}) copy-start(f32[2,512,32]{1,2,0:T(8,128)} %param.27) | copy-start | bytes 393220
  258.4 18.2 %copy-start.11 = (f32[2]{0:T(128)S(1)}, f32[2]{0:T(128)}, u32[]{:S(2)}) copy-start(f32[2]{0:T(128)} %param.31) | copy-start | bytes 28
  270.0 5.2 %collective-permute-start.3 = (bf16[512,64]{0,1:T(8,128)(2,1)S(1)}, bf16[512,64]{0,1:T(8,128)(2,1)S(1)}, u32[]{:S(2)}, u32[]{:S(2)}) collective-permute-start(bf16[512,64]{0,1:T(8,128)(2,1)S(1)} %get-tuple-element.23), channel_id=1, source_target_pairs={{0,8},{4,12},{8,0},{12,4},{1,9},{5,13},{9,1},{13,5},{2,10},{6,14},... | collective-permute-start | bytes 196616 | tf_op jit(solution)/shard_map/ppermute | solution.py:193
  275.3 1.3 collective-permute-start.4
Sparse Core Ops, SparseCore 0:
  31.3 45.0 all-gather.5
  78.2 57.0 all-gather.9
  142.8 43.8 all-gather.7
  213.8 44.6 reduce-scatter.1

commit v2 on v1

--- a/solution.py
+++ b/solution.py
@@ -43,7 +43,7 @@
         acc_in, top_in = refs[:2]
         refs = refs[2:]
     if last:
-        limit_ref, tk_ref, tv_ref = refs[:3]
+        live_ref, tk_ref, tv_ref = refs[:3]
         refs = refs[3:]
     q = q_ref[...]
     lane = lax.broadcasted_iota(jnp.int32, (1, PAIR), 1)
@@ -54,8 +54,7 @@
         qh = jnp.where(own, q, jnp.zeros_like(q))
         pieces = [(k_ref[...], v_ref[...], None)]
         if last:
-            slot = lax.broadcasted_iota(jnp.int32, (1, tk_ref.shape[0]), 1)
-            pieces.append((tk_ref[...], tv_ref[...], slot < limit_ref[0]))
+            pieces.append((tk_ref[...], tv_ref[...], live_ref[...] > 0.5))
         scores = []
         top = None if first else top_in[h]
         for k, v, live in pieces:
@@ -101,7 +100,8 @@
     if last:
         args += list(text)
         t_spec = pl.BlockSpec((text[1].shape[0], PAIR), lambda h, i: (0, h))
-        specs += [pl.BlockSpec(memory_space=pltpu.SMEM), t_spec, t_spec]
+        live_spec = pl.BlockSpec(text[0].shape, lambda h, i: (0, 0))
+        specs += [live_spec, t_spec, t_spec]
         out_shape = jax.ShapeDtypeStruct((rows, width), jnp.bfloat16)
         out_specs = q_spec
     else:
@@ -122,6 +122,182 @@
     )(*args)
 
 
+MESH = pl.DeviceIdType.MESH
+CHUNKS = 4
+
+
+def remote(src, dst, send, recv, target):
+    return pltpu.make_async_remote_copy(
+        src_ref=src, dst_ref=dst, send_sem=send, recv_sem=recv,
+        device_id=target, device_id_type=MESH,
+    )
+
+
+def gather_kernel(S, B, img, txt, out, tout, s_own, r_own, s_swap, r_swap, s_fwd, r_fwd,
+                  s_txt, r_txt, s_tf, r_tf, local):
+    s, b, c = lax.axis_index("seq"), lax.axis_index("blk"), lax.axis_index("cfg")
+    group = S // 2
+    p = s // group
+    sp = (s + group) % S
+    n, w = img.shape[1:]
+    tn = txt.shape[1]
+    step = n // CHUNKS
+    cols = pl.ds(pl.multiple_of(b * w, w), w)
+    barrier = pltpu.get_barrier_semaphore()
+    for d in range(1, S):
+        pl.semaphore_signal(barrier, inc=1, device_id=(c, (s + d) % S, b), device_id_type=MESH)
+    for d in range(1, B):
+        pl.semaphore_signal(barrier, inc=1, device_id=(c, s, (b + d) % B), device_id_type=MESH)
+    pl.semaphore_wait(barrier, S + B - 2)
+
+    swaps = []
+    for j in range(CHUNKS):
+        swaps.append(remote(
+            img.at[1 - p, pl.ds(j * step, step)], out.at[pl.ds(n + j * step, step), cols],
+            s_swap.at[j], r_swap.at[j], (c, sp, b)))
+        swaps[-1].start()
+    texts = []
+    here = pl.ds(pl.multiple_of(s * tn, tn), tn)
+    for d in range(1, S):
+        t = (s + d) % S
+        texts.append(remote(
+            txt.at[t // group], tout.at[here, cols], s_txt.at[d - 1], r_txt.at[d - 1], (c, t, b)))
+        texts[-1].start()
+    own = []
+    for d in range(1, B):
+        own.append(remote(
+            img.at[p], out.at[pl.ds(0, n), cols], s_own.at[d - 1], r_own.at[d - 1],
+            (c, s, (b + d) % B)))
+        own[-1].start()
+    keep = pltpu.make_async_copy(img.at[p], out.at[pl.ds(0, n), cols], local.at[0])
+    keep.start()
+    keep_text = pltpu.make_async_copy(txt.at[p], tout.at[here, cols], local.at[1])
+    keep_text.start()
+    keep_text.wait()
+    for copy in texts:
+        copy.wait()
+    spread = []
+    for d in range(1, B):
+        spread.append(remote(
+            tout.at[:, cols], tout.at[:, cols], s_tf.at[d - 1], r_tf.at[d - 1],
+            (c, s, (b + d) % B)))
+        spread[-1].start()
+    for j in range(CHUNKS):
+        swaps[j].wait()
+        part = out.at[pl.ds(n + j * step, step), cols]
+        for d in range(1, B):
+            spread.append(remote(
+                part, part, s_fwd.at[j, d - 1], r_fwd.at[j, d - 1], (c, s, (b + d) % B)))
+            spread[-1].start()
+    keep.wait()
+    for copy in own + spread:
+        copy.wait()
+
+
+def gather_tokens(img, txt, S, B):
+    n, w = img.shape[1:]
+    tn = txt.shape[1]
+    dma = pltpu.SemaphoreType.DMA
+    shapes = [(B - 1,)] * 2 + [(CHUNKS,)] * 2 + [(CHUNKS, B - 1)] * 2 + [(S - 1,)] * 2 + [(B - 1,)] * 2 + [(2,)]
+    return pl.pallas_call(
+        functools.partial(gather_kernel, S, B),
+        out_shape=[
+            jax.ShapeDtypeStruct((2 * n, B * w), jnp.bfloat16),
+            jax.ShapeDtypeStruct((S * tn, B * w), jnp.bfloat16),
+        ],
+        in_specs=[pl.BlockSpec(memory_space=pl.ANY)] * 2,
+        out_specs=[pl.BlockSpec(memory_space=pl.ANY)] * 2,
+        scratch_shapes=[dma(shape) for shape in shapes],
+        compiler_params=pltpu.CompilerParams(collective_id=0, has_side_effects=True),
+    )(img, txt)
+
+
+def tail_kernel(S, B, vel, par, out, peak, inbox, box, tops, s_in, r_in, s_box, r_box, s_top, r_top):
+    s, b, c = lax.axis_index("seq"), lax.axis_index("blk"), lax.axis_index("cfg")
+    group, side = S // 2, B // 2
+    p = s // group
+    high = b // side
+    t = (s + group * high) % S
+    me = c * S + s
+    barrier = pltpu.get_barrier_semaphore()
+    for d in range(1, 2 * S):
+        o = (me + d) % (2 * S)
+        pl.semaphore_signal(barrier, inc=1, device_id=(o // S, o % S, b), device_id_type=MESH)
+    for d in range(1, B):
+        pl.semaphore_signal(barrier, inc=1, device_id=(c, s, (b + d) % B), device_id_type=MESH)
+    pl.semaphore_wait(barrier, 2 * S - 1 + B - 1)
+
+    across = remote(vel.at[1 - c], inbox.at[c], s_in.at[0], r_in.at[0], (1 - c, t, b))
+    across.start()
+
+    @pl.when(high == 0)
+    def _():
+        inbox[c] = vel[c]
+
+    @pl.when(high == 1)
+    def _():
+        same = remote(vel.at[c], inbox.at[c], s_in.at[1], r_in.at[1], (c, (s + group) % S, b))
+        same.start()
+        same.wait()
+
+    across.wait()
+    cond = inbox[0].astype(jnp.float32)
+    uncond = inbox[1].astype(jnp.float32)
+    box[b] = par[1:2] * (uncond + par[0:1] * (cond - uncond))
+    sends = []
+    for d in range(1, B):
+        sends.append(remote(
+            box.at[b], box.at[b], s_box.at[d - 1], r_box.at[d - 1], (c, s, (b + d) % B)))
+        sends[-1].start()
+    for copy in sends:
+        copy.wait()
+    tall = []
+    width = box.shape[2]
+    for k in range(2):
+        which = p if k == 0 else 1 - p
+        top = None
+        for j in range(side):
+            part = box[k * side + j]
+            out[which, :, j * width:(j + 1) * width] = part
+            value = jnp.max(jnp.abs(part), axis=(0, 1), keepdims=True)
+            top = value if top is None else jnp.maximum(top, value)
+        tall.append(top)
+    row = lax.broadcasted_iota(jnp.int32, (8, 128), 0)
+    tops[me] = jnp.where(row == p, tall[0], tall[1])
+    sends = []
+    for d in range(1, 2 * S):
+        o = (me + d) % (2 * S)
+        sends.append(remote(
+            tops.at[me], tops.at[me], s_top.at[d - 1], r_top.at[d - 1], (o // S, o % S, b)))
+        sends[-1].start()
+    for copy in sends:
+        copy.wait()
+    peak[...] = jnp.max(tops[...], axis=0)
+
+
+def finish(vel, par, S, B):
+    _, chans, width = vel.shape
+    dma = pltpu.SemaphoreType.DMA
+    vmem = pl.BlockSpec(memory_space=pltpu.VMEM)
+    return pl.pallas_call(
+        functools.partial(tail_kernel, S, B),
+        out_shape=[
+            jax.ShapeDtypeStruct((2, chans, width * B // 2), jnp.float32),
+            jax.ShapeDtypeStruct((8, 128), jnp.float32),
+        ],
+        in_specs=[vmem] * 2,
+        out_specs=[vmem] * 2,
+        scratch_shapes=[
+            pltpu.VMEM((2, chans, width), jnp.bfloat16),
+            pltpu.VMEM((B, chans, width), jnp.float32),
+            pltpu.VMEM((2 * S, 8, 128), jnp.float32),
+            dma((2,)), dma((2,)), dma((B - 1,)), dma((B - 1,)),
+            dma((2 * S - 1,)), dma((2 * S - 1,)),
+        ],
+        compiler_params=pltpu.CompilerParams(collective_id=1, has_side_effects=True),
+    )(vel, par)
+
+
 def per_device(
     img_hidden, txt_hidden, img_mod, txt_mod, out_mod, w_qkv, w_txt_kv, w_out,
     w_fc1, w_fc2, w_proj, latent, lengths, t_index, stride, guide,
@@ -137,16 +313,9 @@
     def pick(values):
         return lax.dynamic_index_in_dim(values, prompt, 0, keepdims=False)
 
-    def other(values):
-        return lax.dynamic_index_in_dim(values, 1 - prompt, 0, keepdims=False)
-
-    swap = [(i, (i + group) % seq_size) for i in range(seq_size)]
-    swapped = lax.ppermute(other(img_hidden[0]), "seq", swap)
-    mine = jnp.concatenate([pick(img_hidden[0]), swapped], axis=0)
-    image = lax.all_gather(mine, "blk", axis=1, tiled=True)
-    text = lax.all_gather(txt_hidden[0], "blk", axis=2, tiled=True)
-    text = lax.all_gather(text, "seq", axis=1, tiled=True)
-    text = pick(text)
+    slots = txt_hidden.shape[2]
+    padded = jnp.pad(txt_hidden[0], ((0, 0), (0, -slots % 16), (0, 0)))
+    image, text = gather_tokens(img_hidden[0], padded, seq_size, blk_size)
 
     mod = pick(img_mod[0])
     tmod = pick(txt_mod[0])
@@ -162,18 +331,24 @@
         pieces.append((lax.ppermute(keys, "seq", turn), lax.ppermute(values, "seq", turn)))
     queries = dot(attn_in, w_qkv[0]).astype(jnp.bfloat16)
     text_norm = modulate(text, tmod[0:1], tmod[1:2])
-    slots = text.shape[0]
-    text_norm = jnp.pad(text_norm, ((0, -slots % TEXT_PAD), (0, 0)))
+    extra = -text.shape[0] % TEXT_PAD
+    text_norm = jnp.pad(text_norm, ((0, extra), (0, 0)))
     text_keys = dot(text_norm, w_txt_kv[0]).astype(jnp.bfloat16)
     text_values = dot(text_norm, w_txt_kv[1]).astype(jnp.bfloat16)
-    limit = pick(lengths[0])[None]
-
-    full_out = lax.all_gather(w_out, "blk", axis=0, tiled=True)
-    full_proj = lax.all_gather(w_proj, "blk", axis=0, tiled=True)
+    at = jnp.arange(text_norm.shape[0], dtype=jnp.int32)
+    each = padded.shape[1]
+    live = (at % each < slots) & (at // each * slots + at % each < pick(lengths[0]))
+    live = (live & (at < text.shape[0])).astype(jnp.float32)[None]
+
+    weights = lax.all_gather(
+        jnp.concatenate([w_out, w_proj], axis=1), "blk", axis=0, tiled=True
+    )
+    model_width = w_out.shape[1]
+    full_out, full_proj = weights[:, :model_width], weights[:, model_width:]
 
     state = None
     for at, (k, v) in enumerate(pieces):
-        tail = (limit, text_keys, text_values) if at == len(pieces) - 1 else None
+        tail = (live, text_keys, text_values) if at == len(pieces) - 1 else None
         state = attend_piece(queries, k, v, state, tail)
     attended = lax.all_gather(state, "blk", axis=1, tiled=True)
     resid_one = (image.astype(jnp.float32) + mod[2:3] * dot(attended, full_out)).astype(
@@ -187,23 +362,16 @@
     resid_own = lax.dynamic_slice_in_dim(resid_one, blk_at * own_rows, own_rows, 0)
     resid_two = (resid_own.astype(jnp.float32) + mod[5:6] * mlp_sum).astype(jnp.bfloat16)
     final_in = modulate(resid_two, fmod[0:1], fmod[1:2])
-    velocity = dot(final_in, full_proj).astype(jnp.bfloat16)
-
-    velocity = lax.all_gather(velocity, "blk", axis=0, tiled=True)
-    back = lax.ppermute(velocity[img_rows:], "seq", swap)
-    here = velocity[:img_rows]
-    both = jnp.where(prompt == 0, jnp.stack([here, back]), jnp.stack([back, here]))
-    width = latent.shape[2]
-    outgoing = lax.dynamic_slice_in_dim(both, (1 - half) * width, width, 2)
-    own = lax.dynamic_slice_in_dim(both, half * width, width, 2).astype(jnp.float32)
-    arrived = lax.ppermute(outgoing, "cfg", [(0, 1), (1, 0)]).astype(jnp.float32)
-    cond = jnp.where(half == 0, own, arrived)
-    uncond = jnp.where(half == 0, arrived, own)
-    guided = uncond + guide[:, None, None] * (cond - uncond)
+    velocity = lax.dot_general(
+        full_proj, final_in, (((0,), (1,)), ((), ())), preferred_element_type=jnp.float32
+    ).astype(jnp.bfloat16)
+    velocity = velocity.reshape(2, velocity.shape[0] // 2, own_rows)
     step_size = noise_level(t_index + stride) - noise_level(t_index)
-    update = step_size[:, None, None] * guided
-    peak = lax.pmax(jnp.max(jnp.abs(update), axis=(1, 2)), ("cfg", "seq"))
-    return (latent + update, peak)
+    chunk_prompt = jnp.where(blk_at < blk_size // 2, prompt, 1 - prompt)
+    par = jnp.stack([guide[chunk_prompt], step_size[chunk_prompt]])
+    par = jnp.broadcast_to(par[:, None], (2, own_rows))
+    update, peak = finish(velocity, par, seq_size, blk_size)
+    return (latent + update.transpose(0, 2, 1), peak[:2, 0])
 
 
 def solution(mesh):

time: 302 us -> 332 us (1.099)
  blocking collectives: 67.8 us -> 0 us
  Pallas kernels: 36.9 us -> 103 us
  waiting for transfers between devices: 125 us -> 155 us
  starting transfers between devices: 9.13 us -> 2.45 us
  other arithmetic: 10.9 us -> 15.3 us
    pallas_call x0 -> x2, Pallas kernels: none -> 66.9 us  [the longest x1 51.5 us: gather_tokens(): pl.pallas_call(functools.partial(gather_kernel, S, B), out_shape=[jax.Sha...]
    all_gather x2 -> x1, waiting for transfers between devices: 9.82 us -> 62.2 us  [per_device(): lax.all_gather(jnp.concatenate([w_out, w_proj], axis=1), 'blk', axis=0, t...]
    all_gather x4 -> x0, blocking collectives: 49.9 us -> none  [the longest x1 21.6 us: per_device(): text = lax.all_gather(text, 'seq', axis=1, tiled=True)]
    ppermute x3 -> x0, waiting for transfers between devices: 21.5 us -> none  [the longest x1 17.5 us: per_device(): swapped = lax.ppermute(other(img_hidden[0]), 'seq', swap)]
    pmax x1 -> x0, blocking collectives: 17.9 us -> none  [per_device(): peak = lax.pmax(jnp.max(jnp.abs(update), axis=(1, 2)), ('cfg', 'seq'))]
    reduce_scatter x1, waiting for transfers between devices: 33.9 us -> 40.9 us  [per_device(): lax.psum_scatter(dot(hidden_units, w_fc2).astype(jnp.bfloat16), 'blk', sc...]
    ppermute x3 -> x0, starting transfers between devices: 6.63 us -> none  [the longest x1 4.1 us: per_device(): swapped = lax.ppermute(other(img_hidden[0]), 'seq', swap)]
    ppermute x1, waiting for transfers between devices: 14.9 us -> 11.5 us  [per_device(): lax.ppermute(values, 'seq', turn)]
  transfers between devices with their start and end apart: 9 -> 5, of which waited for: 7 -> 4; matrix products, arithmetic and copies ran while one was open for 5% -> 4% of each run, Pallas kernels for 12% -> 4%
where the time goes in v2:
time: 332 us; the launch traced here: 331 us
  waiting for transfers between devices  155 us (47%)
  Pallas kernels  103 us (31%)
  matrix products  32.9 us (10%)
  other arithmetic  15.3 us (5%)
  between operations  14.1 us (4%)
  local copies, waits for them, and re-layouts  8.35 us (3%)
    all_gather x1, waiting for transfers between devices, per_device(): lax.all_gather(jnp.concatenate([w_out, w_proj], axis=1), 'blk', axis=0, t...  62.2 us
    pallas_call x1, Pallas kernels, gather_tokens(): pl.pallas_call(functools.partial(gather_kernel, S, B), out_shape=[jax.Sha...  51.5 us
    reduce_scatter x1, waiting for transfers between devices, per_device(): lax.psum_scatter(dot(hidden_units, w_fc2).astype(jnp.bfloat16), 'blk', sc...  40.9 us
    all_gather x1, waiting for transfers between devices, per_device(): attended = lax.all_gather(state, 'blk', axis=1, tiled=True)  40.7 us
    pallas_call x2, Pallas kernels, attend_piece(): pl.pallas_call(functools.partial(attend_kernel, first, last), grid=(pairs...  36 us
    dot_general x7, matrix products, dot(): return jnp.dot(a, b, preferred_element_type=jnp.float32)  30.8 us
    pallas_call x1, Pallas kernels, finish(): pl.pallas_call(functools.partial(tail_kernel, S, B), out_shape=[jax.Shape...  15.4 us
    ppermute x1, waiting for transfers between devices, per_device(): lax.ppermute(values, 'seq', turn)  11.5 us
  transfers between devices with their start and end apart: 5, of which 4 were waited for; matrix products, arithmetic and copies ran while one was open for 4% of the time, Pallas kernels for 4%

profile of v2, /device:TPU:0, one launch (start us, length us, event | category | flops | bytes accessed | tf_op | source)
XLA Modules:
  0.0 331.2 jit_solution(11609172568342298868)
XLA Ops:
  7.2 0.0 copy-start
  7.2 0.0 all-gather.5.cloned.1.call-start
  7.2 1.5 pad.8.txt
  8.7 51.5 %shard_map.167 = (bf16[1024,1536]{1,0:T(8,128)(2,1)}, bf16[192,1536]{1,0:T(8,128)(2,1)}) custom-call(bf16[2,512,384]{2,1,0:T(8,128)(2,1)} %bitcast.59, bf16[2,48,384]{2,1,0:T(8,128)(2,1)} %pad.8.txt), custom_call_target="tpu_custom_call" | custom-call | tf_op jit(solution)/shard_map/pallas_call | solution.py:202
  60.2 0.0 copy-start.1
  60.2 0.0 copy-start.6
  60.2 2.5 convert_reduce_fusion
  62.7 0.3 copy-done.1
  63.0 1.0 fusion.4
  64.0 0.0 copy-done.6
  64.0 0.1 fusion.81
  64.1 0.0 copy-start.9
  64.2 1.5 fusion.7
  65.7 0.5 copy-done.9
  66.1 1.8 convolution_convert_fusion.2.refs_1_
  67.9 0.0 copy-start.7
  68.0 0.0 copy-start.10
  68.0 1.3 collective-permute-start
  69.3 1.8 convolution_convert_fusion.1.refs_2_
  71.1 0.8 collective-permute-start.1
  72.0 0.0 copy-done.2
  72.0 0.2 convert_reduce_fusion.3
  72.1 0.3 fusion.48
  72.4 0.4 fusion.51
  72.9 0.6 fusion.64.refs_6_
  73.5 0.6 fusion.67.refs_7_
  74.0 0.0 copy-done
  74.0 0.6 constant_dynamic-slice_fusion
  74.6 0.7 and_convert_fusion.refs_5_
  75.3 1.8 convolution_convert_fusion.3.refs_0_
  77.1 14.4 %shard_map.168 = (f32[6,1024,128]{2,1,0:T(8,128)S(1)}, f32[6,1024,128]{2,1,0:T(8,128)S(1)}) custom-call(bf16[1024,384]{1,0:T(8,128)(2,1)S(1)} %convolution_convert_fusion.3.refs_0_, bf16[1024,384]{1,0:T(8,128)(2,1)S(1)} %convolution_convert_fusion.2.refs_1_, bf16[1024,384]{1,0:T(8,128)(2,1)S(1)} %convolution_convert_fusion.1.refs_2_), custom_call_target="tpu_custom_call" | custom-call | flops 3221225472 | bytes 3145728 | tf_op jit(solution)/shard_map/pallas_call | solution.py:110
  91.5 0.0 collective-permute-done.refs_1_
  91.5 11.5 %collective-permute-done.1.refs_2_ = bf16[1024,384]{1,0:T(8,128)(2,1)S(1)} collective-permute-done((bf16[1024,384]{1,0:T(8,128)(2,1)S(1)}, bf16[1024,384]{1,0:T(8,128)(2,1)S(1)}, u32[]{:S(2)}, u32[]{:S(2)}) %collective-permute-start.1) | collective-permute-done | bytes 786464 | tf_op jit(solution)/shard_map/ppermute | solution.py:331
  103.0 21.6 %shard_map.169 = bf16[1024,384]{1,0:T(8,128)(2,1)} custom-call(bf16[1024,384]{1,0:T(8,128)(2,1)S(1)} %convolution_convert_fusion.3.refs_0_, bf16[1024,384]{1,0:T(8,128)(2,1)S(1)} %collective-permute-done.refs_1_, bf16[1024,384]{1,0:T(8,128)(2,1)S(1)} %collective-permute-done.1.refs_2_, f32[6,1024,128]{2,1,0:T(8,128)S(1)} %get-tuple-element.9.refs_3_, ...), custom_call_target="tpu_custom_call" | custom-call | flops 3221225472 | bytes 3145728 | tf_op jit(solution)/shard_map/pallas_call | solution.py:110
  124.6 0.0 all-gather.5.cloned.1.call-update
  124.6 0.0 all-gather.3.cloned.1.call-start
  124.6 0.1 copy.20
  124.8 2.5 pad_maximum_fusion
  127.3 0.0 all-gather.3.cloned.1.call-update
  127.3 0.2 reduce-scatter.2.cloned.1.call-start
  127.5 40.7 %all-gather.5.cloned.1.call-done = bf16[1024,1536]{1,0:T(8,128)(2,1)} async-done(((bf16[1024,384]{1,0:T(8,128)(2,1)}), bf16[1024,1536]{1,0:T(8,128)(2,1)}) %all-gather.5.cloned.1.call-update) | async-done | bytes 3145744 | tf_op jit(solution)/shard_map/all_gather | solution.py:353
  168.2 62.2 %all-gather.3.cloned.1.call-done = bf16[1536,1600]{1,0:T(8,128)(2,1)} async-done(((bf16[384,1600]{1,0:T(8,128)(2,1)}), bf16[1536,1600]{1,0:T(8,128)(2,1)}) %all-gather.3.cloned.1.call-update) | async-done | bytes 4915216 | tf_op jit(solution)/shard_map/all_gather | solution.py:343
  230.4 8.4 %convert_reduce_fusion.1 = (f32[1024]{0:T(1024)S(1)}, bf16[1024,1536]{1,0:T(8,128)(2,1)S(1)}) fusion(bf16[1024,1536]{1,0:T(8,128)(2,1)} %all-gather.5.cloned.1.call-done, bf16[1536,1600]{1,0:T(8,128)(2,1)} %all-gather.3.cloned.1.call-done, f32[1536]{0:T(1024)S(1)} %get-tuple-element.18, bf16[1024,1536]{1,0:T(8,128)(2,1)S(1)} %copy-done.1), kind=kOutput, calls=%fused_computation.5 | convolution fusion | flops 4841274368 | bytes 14166016 | tf_op jit(solution)/shard_map/dot_general | solution.py:30
  238.8 1.6 copy-done.3
  240.4 1.0 fusion.8
  241.4 15.9 %convolution_convert_fusion = bf16[1024,1536]{1,0:T(8,128)(2,1)} fusion(bf16[1536,1536]{1,0:T(8,128)(2,1)} %param.25, bf16[1536,1536]{1,0:T(8,128)(2,1)} %param.24, bf16[1024,1536]{1,0:T(8,128)(2,1)} %copy-done.3, f32[1536]{0:T(1024)S(1)} %get-tuple-element.19, f32[1536]{0:T(1024)S(1)} %get-tuple-element.15, f32[1024]{0:T(1024)S(1)} %add_rsqrt_fusion, ...), kind=kOutput, calls=%fused_computation.29 | convolution fusion | flops 9688842240 | bytes 15749120 | tf_op jit(solution)/shard_map/dot_general | solution.py:30
  257.3 0.0 copy-start.8
  257.3 0.0 reduce-scatter.2.cloned.1.call-update
  257.4 0.0 copy-start.4
  257.4 0.6 copy-done.11
  258.0 0.0 copy-done.12
  258.0 0.6 dynamic_slice.30
  258.6 0.0 copy-done.13
  258.6 0.6 dynamic_slice.29
  259.2 1.4 pad_maximum_fusion.1
  260.6 40.9 %reduce-scatter.2.cloned.1.call-done = bf16[256,1536]{1,0:T(8,128)(2,1)} async-done(((bf16[1024,1536]{1,0:T(8,128)(2,1)}), bf16[256,1536]{1,0:T(8,128)(2,1)}) %reduce-scatter.2.cloned.1.call-update) | async-done | bytes 786448 | tf_op jit(solution)/shard_map/reduce_scatter | solution.py:359
  301.5 1.7 convert_reduce_fusion.2
  303.2 0.4 fusion.38
  303.6 2.1 convolution_convert_fusion.4
  305.7 0.7 broadcast_in_dim.2.par
  306.4 15.4 %shard_map.170 = (f32[2,32,512]{2,1,0:T(8,128)}, f32[8,128]{1,0:T(8,128)}) custom-call(bf16[2,32,256]{2,1,0:T(8,128)(2,1)} %bitcast.61, f32[2,256]{1,0:T(2,128)} %broadcast_in_dim.2.par), custom_call_target="tpu_custom_call" | custom-call | tf_op jit(solution)/shard_map/pallas_call | solution.py:282
  321.8 1.3 slice_reduce_fusion
  323.1 0.0 copy-done.4
  323.1 1.6 bitcast_add_fusion
  (21 shorter events, 0.2 us)
Async XLA Ops:
  7.2 66.9 %copy-start = (s32[1,2]{1,0:T(1,128)S(1)}, s32[1,2]{1,0:T(1,128)}, u32[]{:S(2)}) copy-start(s32[1,2]{1,0:T(1,128)} %param.28) | copy-start | bytes 28
  7.2 161.0 %all-gather.5.cloned.1.call-start = ((), (), s32[]{:S(2)}) async-start(), calls=%async_computation.2 | async-start | bytes 3932160 | tf_op jit(solution)/shard_map/all_gather | solution.py:353
  60.2 2.8 copy-start.1
  60.2 3.8 %copy-start.6 = (f32[1,2,6,1536]{3,1,2,0:T(2,128)S(1)}, f32[1,2,6,1536]{3,1,2,0:T(2,128)}, u32[]{:S(2)}) copy-start(f32[1,2,6,1536]{3,1,2,0:T(2,128)} %param.18) | copy-start | bytes 221188
  64.1 2.0 copy-start.9
  67.9 4.0 %copy-start.7 = (f32[1,2,2,1536]{3,2,1,0:T(2,128)S(1)}, f32[1,2,2,1536]{3,2,1,0:T(2,128)}, u32[]{:S(2)}) copy-start(f32[1,2,2,1536]{3,2,1,0:T(2,128)} %param.19) | copy-start | bytes 73732
  67.9 4.0 %copy-start.2 = (bf16[192,1536]{1,0:T(8,128)(2,1)S(1)}, bf16[192,1536]{1,0:T(8,128)(2,1)}, u32[]{:S(2)}) copy-start(bf16[192,1536]{1,0:T(8,128)(2,1)} %get-tuple-element.11) | copy-start | bytes 1769476
  68.0 4.9 %copy-start.10 = (bf16[2,1536,384]{2,1,0:T(8,128)(2,1)S(1)}, bf16[2,1536,384]{2,1,0:T(8,128)(2,1)}, u32[]{:S(2)}) copy-start(bf16[2,1536,384]{2,1,0:T(8,128)(2,1)} %param.22) | copy-start | bytes 7077892
  68.0 23.5 %collective-permute-start = (bf16[1024,384]{1,0:T(8,128)(2,1)S(1)}, bf16[1024,384]{1,0:T(8,128)(2,1)S(1)}, u32[]{:S(2)}, u32[]{:S(2)}) collective-permute-start(bf16[1024,384]{1,0:T(8,128)(2,1)S(1)} %convolution_convert_fusion.2.refs_1_), channel_id=1, source_target_pairs={{0,4},{4,0},{8,12},{12,8},{1,5},{5,1},{9,13},{13,9},{2,6},{6,2},{1... | collective-permute-start | bytes 2359304 | tf_op jit(solution)/shard_map/ppermute | solution.py:331
  71.1 31.9 %collective-permute-start.1 = (bf16[1024,384]{1,0:T(8,128)(2,1)S(1)}, bf16[1024,384]{1,0:T(8,128)(2,1)S(1)}, u32[]{:S(2)}, u32[]{:S(2)}) collective-permute-start(bf16[1024,384]{1,0:T(8,128)(2,1)S(1)} %convolution_convert_fusion.1.refs_2_), channel_id=1, source_target_pairs={{0,4},{4,0},{8,12},{12,8},{1,5},{5,1},{9,13},{13,9},{2,6},{6,2},{1... | collective-permute-start | bytes 2359304 | tf_op jit(solution)/shard_map/ppermute | solution.py:331
  103.0 21.7 %copy-start.5 = (bf16[384,64]{0,1:T(8,128)(2,1)S(1)}, bf16[384,64]{0,1:T(8,128)(2,1)}, u32[]{:S(2)}) copy-start(bf16[384,64]{0,1:T(8,128)(2,1)} %param.26) | copy-start | bytes 147460
  124.6 105.8 %all-gather.3.cloned.1.call-start = ((), (), s32[]{:S(2)}) async-start(), calls=%async_computation.1 | async-start | bytes 6389760 | tf_op jit(solution)/shard_map/all_gather | solution.py:343
  127.3 174.2 %reduce-scatter.2.cloned.1.call-start = ((), (), s32[]{:S(2)}) async-start(), calls=%async_computation.3 | async-start | bytes 3932160 | tf_op jit(solution)/shard_map/reduce_scatter | solution.py:359
  238.8 1.6 copy-start.3
  257.3 0.7 copy-start.11
  257.3 0.7 copy-start.12
  257.3 1.3 copy-start.13
  257.3 1.9 copy-start.8
  257.4 65.8 %copy-start.4 = (f32[2,512,32]{1,2,0:T(8,128)S(1)}, f32[2,512,32]{1,2,0:T(8,128)}, u32[]{:S(2)}) copy-start(f32[2,512,32]{1,2,0:T(8,128)} %param.27) | copy-start | bytes 393220
Sparse Core Ops, SparseCore 0:
  124.7 43.4 all-gather.4
  170.0 60.3 all-gather.2
  257.5 43.9 reduce-scatter.1

commit v3 on v2

--- a/solution.py
+++ b/solution.py
@@ -35,7 +35,31 @@
     return 3.0 * remain / (1.0 + 2.0 * remain)
 
 
-def attend_kernel(first, last, *refs):
+MESH = pl.DeviceIdType.MESH
+CHUNKS = 4
+
+
+def remote(src, dst, send, recv, target):
+    return pltpu.make_async_remote_copy(
+        src_ref=src, dst_ref=dst, send_sem=send, recv_sem=recv,
+        device_id=target, device_id_type=MESH,
+    )
+
+
+def at_ends():
+    h, i = pl.program_id(0), pl.program_id(1)
+    pairs, blocks = pl.num_programs(0), pl.num_programs(1)
+    return h, i, blocks, (h == 0) & (i == 0), (h == pairs - 1) & (i == blocks - 1)
+
+
+def greet(targets):
+    barrier = pltpu.get_barrier_semaphore()
+    for target in targets:
+        pl.semaphore_signal(barrier, inc=1, device_id=target, device_id_type=MESH)
+    pl.semaphore_wait(barrier, len(targets))
+
+
+def attend_kernel(first, last, S, B, steps, *refs):
     refs = list(refs)
     q_ref, k_ref, v_ref = refs[:3]
     refs = refs[3:]
@@ -45,6 +69,59 @@
     if last:
         live_ref, tk_ref, tv_ref = refs[:3]
         refs = refs[3:]
+    s_at, b, c = lax.axis_index("seq"), lax.axis_index("blk"), lax.axis_index("cfg")
+    h_at, i_at, blocks, opening, closing = at_ends()
+    peers = [(c, s_at, (b + d) % B) for d in range(1, B)]
+    if first:
+        w_ref, refs = refs[0], refs[1:]
+        *refs, s_w, r_w, s_x, r_x, w_sem = refs
+        w_full, refs = refs[-1], refs[:-1]
+        depth = w_ref.shape[0]
+        half = depth // 2
+
+        def share(d):
+            rows = pl.ds(pl.multiple_of(b * depth + c * half, half), half)
+            return remote(
+                w_ref.at[pl.ds(pl.multiple_of(c * half, half), half)], w_full.at[rows],
+                s_w.at[d - 1], r_w.at[d - 1], peers[d - 1])
+
+        def cross(d):
+            rows = pl.ds(pl.multiple_of((b + B - d) % B * depth + c * half, half), half)
+            return remote(
+                w_full.at[rows], w_full.at[rows], s_x.at[d - 1], r_x.at[d - 1], (1 - c, s_at, b))
+
+        def keep():
+            rows = pl.ds(pl.multiple_of(b * depth, depth), depth)
+            return pltpu.make_async_copy(w_ref, w_full.at[rows], w_sem.at[0])
+
+        @pl.when(opening)
+        def _():
+            greet(peers + [(1 - c, s_at, b)])
+            for d in range(1, B):
+                share(d).start()
+            keep().start()
+
+    if last:
+        *refs, held, s_o, r_o, l_o = refs
+
+        def place(at):
+            return refs[-1].at[
+                pl.ds(pl.multiple_of(at % steps[1] * Q_ROWS, Q_ROWS), Q_ROWS),
+                pl.ds(pl.multiple_of(b * (steps[0] * PAIR) + at // steps[1] * PAIR, PAIR), PAIR),
+            ]
+
+        def give(at, d):
+            return remote(
+                held.at[at], place(at), s_o.at[d - 1, at], r_o.at[d - 1, at], peers[d - 1])
+
+        def own_copy(at):
+            return pltpu.make_async_copy(held.at[at], place(at), l_o.at[at])
+
+        if not first:
+            @pl.when(opening)
+            def _():
+                greet(peers)
+
     q = q_ref[...]
     lane = lax.broadcasted_iota(jnp.int32, (1, PAIR), 1)
     scale = HEAD ** (-0.5)
@@ -75,25 +152,52 @@
             acc = part if acc is None else acc + part
         results.append((acc, top))
     if last:
-        (out_ref,) = refs
         outs = [acc / pltpu.roll(acc, HEAD, 1) for acc, _ in results]
-        out_ref[...] = jnp.where(lane < HEAD, outs[0], outs[1]).astype(jnp.bfloat16)
+        now = h_at * steps[1] + i_at
+        held[now] = jnp.where(lane < HEAD, outs[0], outs[1]).astype(jnp.bfloat16)
+        for d in range(1, B):
+            give(now, d).start()
+        own_copy(now).start()
+
+        @pl.when(closing)
+        def _():
+            def drain(at, carry):
+                for d in range(1, B):
+                    give(at, d).wait()
+                own_copy(at).wait()
+                return carry
+
+            lax.fori_loop(0, steps[0] * steps[1], drain, 0)
     else:
         acc_out, top_out = refs
         for h in range(2):
             acc_out[h] = results[h][0]
             top_out[h] = results[h][1]
-
-
-def attend_piece(queries, keys, values, state, text):
+    if first:
+        @pl.when(closing)
+        def _():
+            for d in range(1, B):
+                share(d).wait()
+                cross(d).start()
+            for d in range(1, B):
+                cross(d).wait()
+            keep().wait()
+
+
+def attend_piece(queries, keys, values, state, text, weights, S, B):
     rows, width = queries.shape
     count = keys.shape[0]
     pairs = width // PAIR
+    steps = (pairs, rows // Q_ROWS)
+    total = steps[0] * steps[1]
+    dma = pltpu.SemaphoreType.DMA
     first, last = state is None, text is not None
     q_spec = pl.BlockSpec((Q_ROWS, PAIR), lambda h, i: (i, h))
     kv_spec = pl.BlockSpec((count, PAIR), lambda h, i: (0, h))
     s_spec = pl.BlockSpec((2, Q_ROWS, PAIR), lambda h, i: (h, i, 0))
+    anywhere = pl.BlockSpec(memory_space=pl.ANY)
     args, specs = [queries, keys, values], [q_spec, kv_spec, kv_spec]
+    out_shape, out_specs, scratch = [], [], []
     if not first:
         args += list(state)
         specs += [s_spec, s_spec]
@@ -102,35 +206,37 @@
         t_spec = pl.BlockSpec((text[1].shape[0], PAIR), lambda h, i: (0, h))
         live_spec = pl.BlockSpec(text[0].shape, lambda h, i: (0, 0))
         specs += [live_spec, t_spec, t_spec]
-        out_shape = jax.ShapeDtypeStruct((rows, width), jnp.bfloat16)
-        out_specs = q_spec
+        out_shape += [jax.ShapeDtypeStruct((rows, B * width), jnp.bfloat16)]
+        out_specs += [anywhere]
+        scratch += [
+            pltpu.VMEM((total, Q_ROWS, PAIR), jnp.bfloat16),
+            dma((B - 1, total)), dma((B - 1, total)), dma((total,)),
+        ]
     else:
-        out_shape = [jax.ShapeDtypeStruct((2 * pairs, rows, PAIR), jnp.float32)] * 2
-        out_specs = [s_spec, s_spec]
+        out_shape += [jax.ShapeDtypeStruct((2 * pairs, rows, PAIR), jnp.float32)] * 2
+        out_specs += [s_spec, s_spec]
+    if first:
+        args.append(weights)
+        specs.append(anywhere)
+        depth, across = weights.shape
+        out_shape.append(jax.ShapeDtypeStruct((B * depth, across), jnp.bfloat16))
+        out_specs.append(anywhere)
+        scratch += [dma((B - 1,))] * 4 + [dma((1,))]
+    reach = {"collective_id": 2 if first else 3, "has_side_effects": True} if first or last else {}
     return pl.pallas_call(
-        functools.partial(attend_kernel, first, last),
-        grid=(pairs, rows // Q_ROWS),
+        functools.partial(attend_kernel, first, last, S, B, steps),
+        grid=steps,
         in_specs=specs,
         out_specs=out_specs,
         out_shape=out_shape,
-        compiler_params=pltpu.CompilerParams(vmem_limit_bytes=40 * 1024 * 1024),
+        scratch_shapes=scratch,
+        compiler_params=pltpu.CompilerParams(vmem_limit_bytes=40 * 1024 * 1024, **reach),
         cost_estimate=pl.CostEstimate(
             flops=8 * rows * count * width,
             bytes_accessed=8 * rows * width,
             transcendentals=rows * count * width // HEAD,
         ),
     )(*args)
-
-
-MESH = pl.DeviceIdType.MESH
-CHUNKS = 4
-
-
-def remote(src, dst, send, recv, target):
-    return pltpu.make_async_remote_copy(
-        src_ref=src, dst_ref=dst, send_sem=send, recv_sem=recv,
-        device_id=target, device_id_type=MESH,
-    )
 
 
 def gather_kernel(S, B, img, txt, out, tout, s_own, r_own, s_swap, r_swap, s_fwd, r_fwd,
@@ -340,17 +446,18 @@
     live = (at % each < slots) & (at // each * slots + at % each < pick(lengths[0]))
     live = (live & (at < text.shape[0])).astype(jnp.float32)[None]
 
-    weights = lax.all_gather(
-        jnp.concatenate([w_out, w_proj], axis=1), "blk", axis=0, tiled=True
-    )
     model_width = w_out.shape[1]
-    full_out, full_proj = weights[:, :model_width], weights[:, model_width:]
-
+    block = jnp.concatenate([w_out, w_proj], axis=1)
+    block = jnp.pad(block, ((0, 0), (0, -block.shape[1] % 128)))
     state = None
     for at, (k, v) in enumerate(pieces):
         tail = (live, text_keys, text_values) if at == len(pieces) - 1 else None
-        state = attend_piece(queries, k, v, state, tail)
-    attended = lax.all_gather(state, "blk", axis=1, tiled=True)
+        state = attend_piece(queries, k, v, state, tail, block, seq_size, blk_size)
+        if at == 0:
+            *state, weights = state
+    (attended,) = state
+    full_out = weights[:, :model_width]
+    full_proj = weights[:, model_width:model_width + w_proj.shape[1]]
     resid_one = (image.astype(jnp.float32) + mod[2:3] * dot(attended, full_out)).astype(
         jnp.bfloat16
     )

time: 332 us -> 253 us (0.76)
  waiting for transfers between devices: 155 us -> 40 us
  Pallas kernels: 103 us -> 141 us
    all_gather x2 -> x0, waiting for transfers between devices: 103 us -> none  [the longest x1 62.2 us: per_device(): lax.all_gather(jnp.concatenate([w_out, w_proj], axis=1), 'blk', axis=0, t...]
    pallas_call x2, Pallas kernels: 36 us -> 73.6 us  [attend_piece(): pl.pallas_call(functools.partial(attend_kernel, first, last, S, B, steps)...]
    ppermute x1, waiting for transfers between devices: 11.5 us -> 0.01 us  [per_device(): lax.ppermute(values, 'seq', turn)]
  transfers between devices with their start and end apart: 5 -> 3, of which waited for: 4 -> 1; matrix products, arithmetic and copies ran while one was open for 4% -> 6% of each run, Pallas kernels for 4% -> 14%
where the time goes in v3:
time: 253 us; the launch traced here: 252 us
  Pallas kernels  141 us (56%)
  waiting for transfers between devices  40 us (16%)
  matrix products  32.2 us (13%)
  other arithmetic  14.5 us (6%)
  between operations  14.4 us (6%)
  local copies, waits for them, and re-layouts  8.2 us (3%)
    pallas_call x2, Pallas kernels, attend_piece(): pl.pallas_call(functools.partial(attend_kernel, first, last, S, B, steps)...  73.6 us
    pallas_call x1, Pallas kernels, gather_tokens(): pl.pallas_call(functools.partial(gather_kernel, S, B), out_shape=[jax.Sha...  51.5 us
    reduce_scatter x1, waiting for transfers between devices, per_device(): lax.psum_scatter(dot(hidden_units, w_fc2).astype(jnp.bfloat16), 'blk', sc...  39.9 us
    dot_general x7, matrix products, dot(): return jnp.dot(a, b, preferred_element_type=jnp.float32)  30.1 us
    pallas_call x1, Pallas kernels, finish(): pl.pallas_call(functools.partial(tail_kernel, S, B), out_shape=[jax.Shape...  15.4 us
  transfers between devices with their start and end apart: 3, of which 1 were waited for; matrix products, arithmetic and copies ran while one was open for 6% of the time, Pallas kernels for 14%

profile of v3, /device:TPU:0, one launch (start us, length us, event | category | flops | bytes accessed | tf_op | source)
XLA Modules:
  0.0 252.0 jit_solution(13166323401909830878)
XLA Ops:
  7.2 0.0 copy-start
  7.2 0.0 reduce-scatter.2.cloned.1.call-start
  7.2 1.5 pad.12.txt
  8.7 51.5 %shard_map.167 = (bf16[1024,1536]{1,0:T(8,128)(2,1)}, bf16[192,1536]{1,0:T(8,128)(2,1)}) custom-call(bf16[2,512,384]{2,1,0:T(8,128)(2,1)} %bitcast.59, bf16[2,48,384]{2,1,0:T(8,128)(2,1)} %pad.12.txt), custom_call_target="tpu_custom_call" | custom-call | tf_op jit(solution)/shard_map/pallas_call | solution.py:308
  60.2 0.0 copy-start.1
  60.2 0.0 copy-start.6
  60.2 0.0 copy-start.10
  60.2 2.5 convert_reduce_fusion
  62.8 0.3 copy-done.1
  63.0 1.0 fusion.4
  64.0 0.0 copy-done.6
  64.0 0.0 copy-done.10
  64.0 0.7 fusion.84
  64.8 1.5 fusion.7
  66.2 0.5 copy-done.12
  66.8 1.8 convolution_convert_fusion.2.refs_1_
  68.5 0.0 copy-start.3
  68.6 0.0 copy-start.13
  68.6 1.3 collective-permute-start
  69.9 0.0 copy-done.4
  69.9 1.8 convolution_convert_fusion.1.refs_2_
  71.7 0.8 collective-permute-start.1
  72.5 0.0 copy-done.3
  72.5 0.2 convert_reduce_fusion.3
  72.7 0.3 fusion.51
  73.0 0.4 fusion.54
  73.4 0.0 copy-done.13
  73.4 0.6 fusion.67.refs_6_
  74.0 0.6 fusion.70.refs_7_
  74.6 1.5 copy.21
  76.1 0.6 constant_dynamic-slice_fusion
  76.7 1.4 fusion.50.refs_3_
  78.1 0.7 and_convert_fusion.refs_5_
  78.8 4.0 %convolution_convert_fusion.3.refs_0_ = bf16[1024,384]{1,0:T(8,128)(2,1)S(1)} fusion(bf16[1024,1536]{1,0:T(8,128)(2,1)} %copy-done.4, bf16[3,1536,384]{2,1,0:T(8,128)(2,1)} %param.21), kind=kOutput, calls=%fused_computation.57 | convolution fusion | flops 1208352768 | bytes 5111808 | tf_op jit(solution)/shard_map/dot_general | solution.py:30
  82.8 34.1 %shard_map.168 = (f32[6,1024,128]{2,1,0:T(8,128)S(1)}, f32[6,1024,128]{2,1,0:T(8,128)S(1)}, bf16[1536,1664]{1,0:T(8,128)(2,1)}) custom-call(bf16[1024,384]{1,0:T(8,128)(2,1)S(1)} %convolution_convert_fusion.3.refs_0_, bf16[1024,384]{1,0:T(8,128)(2,1)S(1)} %convolution_convert_fusion.2.refs_1_, bf16[1024,384]{1,0:T(8,128)(2,1)S(1)} %convolution_convert_fusion.1.refs_2_, ...), custom_call_target="tpu_custom_call" | custom-call | flops 3221225472 | bytes 3145728 | tf_op jit(solution)/shard_map/pallas_call | solution.py:226
  116.9 0.0 collective-permute-done.refs_1_
  116.9 0.0 collective-permute-done.1.refs_2_
  116.9 0.0 copy-start.2
  117.0 0.0 copy-start.9
  117.0 0.0 copy-start.17
  117.0 39.5 %shard_map.169 = bf16[1024,1536]{1,0:T(8,128)(2,1)S(1)} custom-call(bf16[1024,384]{1,0:T(8,128)(2,1)S(1)} %convolution_convert_fusion.3.refs_0_, bf16[1024,384]{1,0:T(8,128)(2,1)S(1)} %collective-permute-done.refs_1_, bf16[1024,384]{1,0:T(8,128)(2,1)S(1)} %collective-permute-done.1.refs_2_, f32[6,1024,128]{2,1,0:T(8,128)S(1)} %get-tuple-element.11.refs_3_, ...), custom_call_target="tpu_custom_call" | custom-call | flops 3221225472 | bytes 3145728 | tf_op jit(solution)/shard_map/pallas_call | solution.py:226
  156.5 0.0 copy-done.2
  156.5 0.0 copy-done.9
  156.5 0.0 copy-done.17
  156.5 5.8 %convert_reduce_fusion.1 = (f32[1024]{0:T(1024)S(1)}, bf16[1024,1536]{1,0:T(8,128)(2,1)S(1)}) fusion(bf16[1024,1536]{1,0:T(8,128)(2,1)S(1)} %shard_map.169, bf16[1536,1664]{1,0:T(8,128)(2,1)S(1)} %copy-done.17, f32[1536]{0:T(1024)S(1)} %copy-done.9, bf16[1024,1536]{1,0:T(8,128)(2,1)S(1)} %copy-done.2), kind=kOutput, calls=%fused_computation.5 | convolution fusion | flops 4841274368 | bytes 14168064 | tf_op jit(solution)/shard_map/dot_general | solution.py:30
  162.3 0.0 copy-start.7
  162.3 0.0 copy-start.8
  162.3 1.0 fusion.8
  163.3 15.6 %convolution_convert_fusion = bf16[1024,1536]{1,0:T(8,128)(2,1)} fusion(bf16[1536,1536]{1,0:T(8,128)(2,1)} %param.25, bf16[1536,1536]{1,0:T(8,128)(2,1)} %param.24, bf16[1024,1536]{1,0:T(8,128)(2,1)S(1)} %get-tuple-element.29, f32[1536]{0:T(1024)S(1)} %copy-done.8, f32[1536]{0:T(1024)S(1)} %copy-done.7, f32[1024]{0:T(1024)S(1)} %add_rsqrt_fusion, ...), kind=kOutput, calls=%fused_computation.29 | convolution fusion | flops 9688842240 | bytes 15749120 | tf_op jit(solution)/shard_map/dot_general | solution.py:30
  178.9 0.0 reduce-scatter.2.cloned.1.call-update
  179.0 0.0 copy-start.5
  179.0 0.6 copy-done.14
  179.6 0.0 copy-done.15
  179.6 0.6 dynamic_slice.30
  180.2 0.6 dynamic_slice.29
  180.8 1.4 pad_maximum_fusion
  182.2 39.9 %reduce-scatter.2.cloned.1.call-done = bf16[256,1536]{1,0:T(8,128)(2,1)} async-done(((bf16[1024,1536]{1,0:T(8,128)(2,1)}), bf16[256,1536]{1,0:T(8,128)(2,1)}) %reduce-scatter.2.cloned.1.call-update) | async-done | bytes 786448 | tf_op jit(solution)/shard_map/reduce_scatter | solution.py:466
  222.1 1.5 convert_reduce_fusion.2
  223.6 0.4 fusion.40
  224.0 2.1 convolution_convert_fusion.4
  226.1 0.7 broadcast_in_dim.2.par
  226.8 15.4 %shard_map.170 = (f32[2,32,512]{2,1,0:T(8,128)}, f32[8,128]{1,0:T(8,128)}) custom-call(bf16[2,32,256]{2,1,0:T(8,128)(2,1)} %bitcast.61, f32[2,256]{1,0:T(2,128)} %broadcast_in_dim.2.par), custom_call_target="tpu_custom_call" | custom-call | tf_op jit(solution)/shard_map/pallas_call | solution.py:388
  242.3 1.3 slice_reduce_fusion
  243.6 1.6 bitcast_add_fusion
  (22 shorter events, 0.1 us)
Async XLA Ops:
  7.2 69.0 %copy-start = (s32[1,2]{1,0:T(1,128)S(1)}, s32[1,2]{1,0:T(1,128)}, u32[]{:S(2)}) copy-start(s32[1,2]{1,0:T(1,128)} %param.28) | copy-start | bytes 28
  7.2 214.9 %reduce-scatter.2.cloned.1.call-start = ((), (), s32[]{:S(2)}) async-start(), calls=%async_computation.1 | async-start | bytes 3932160 | tf_op jit(solution)/shard_map/reduce_scatter | solution.py:466
  60.2 2.8 %copy-start.1 = (bf16[1024,1536]{1,0:T(8,128)(2,1)S(1)}, bf16[1024,1536]{1,0:T(8,128)(2,1)}, u32[]{:S(2)}) copy-start(bf16[1024,1536]{1,0:T(8,128)(2,1)} %get-tuple-element.9) | copy-start | bytes 9437188
  60.2 3.8 %copy-start.6 = (f32[1,2,6,1536]{3,1,2,0:T(2,128)S(1)}, f32[1,2,6,1536]{3,1,2,0:T(2,128)}, u32[]{:S(2)}) copy-start(f32[1,2,6,1536]{3,1,2,0:T(2,128)} %param.18) | copy-start | bytes 221188
  60.2 3.8 %copy-start.10 = (f32[1,2,2,1536]{3,2,1,0:T(2,128)S(1)}, f32[1,2,2,1536]{3,2,1,0:T(2,128)}, u32[]{:S(2)}) copy-start(f32[1,2,2,1536]{3,2,1,0:T(2,128)} %param.19) | copy-start | bytes 73732
  64.8 2.0 copy-start.12
  66.8 3.1 %copy-start.4 = (bf16[1024,1536]{1,0:T(8,128)(2,1)}, bf16[1024,1536]{1,0:T(8,128)(2,1)S(1)}, u32[]{:S(2)}) copy-start(bf16[1024,1536]{1,0:T(8,128)(2,1)S(1)} %fusion.7) | copy-start | bytes 9437188
  68.5 4.0 %copy-start.3 = (bf16[192,1536]{1,0:T(8,128)(2,1)S(1)}, bf16[192,1536]{1,0:T(8,128)(2,1)}, u32[]{:S(2)}) copy-start(bf16[192,1536]{1,0:T(8,128)(2,1)} %get-tuple-element.13) | copy-start | bytes 1769476
  68.6 4.9 %copy-start.13 = (bf16[2,1536,384]{2,1,0:T(8,128)(2,1)S(1)}, bf16[2,1536,384]{2,1,0:T(8,128)(2,1)}, u32[]{:S(2)}) copy-start(bf16[2,1536,384]{2,1,0:T(8,128)(2,1)} %param.22) | copy-start | bytes 7077892
  68.6 48.4 %collective-permute-start = (bf16[1024,384]{1,0:T(8,128)(2,1)S(1)}, bf16[1024,384]{1,0:T(8,128)(2,1)S(1)}, u32[]{:S(2)}, u32[]{:S(2)}) collective-permute-start(bf16[1024,384]{1,0:T(8,128)(2,1)S(1)} %convolution_convert_fusion.2.refs_1_), channel_id=1, source_target_pairs={{0,4},{4,0},{8,12},{12,8},{1,5},{5,1},{9,13},{13,9},{2,6},{6,2},{1... | collective-permute-start | bytes 2359304 | tf_op jit(solution)/shard_map/ppermute | solution.py:437
  71.7 45.3 %collective-permute-start.1 = (bf16[1024,384]{1,0:T(8,128)(2,1)S(1)}, bf16[1024,384]{1,0:T(8,128)(2,1)S(1)}, u32[]{:S(2)}, u32[]{:S(2)}) collective-permute-start(bf16[1024,384]{1,0:T(8,128)(2,1)S(1)} %convolution_convert_fusion.1.refs_2_), channel_id=1, source_target_pairs={{0,4},{4,0},{8,12},{12,8},{1,5},{5,1},{9,13},{13,9},{2,6},{6,2},{1... | collective-permute-start | bytes 2359304 | tf_op jit(solution)/shard_map/ppermute | solution.py:437
  116.9 39.5 %copy-start.2 = (bf16[1024,1536]{1,0:T(8,128)(2,1)S(1)}, bf16[1024,1536]{1,0:T(8,128)(2,1)}, u32[]{:S(2)}) copy-start(bf16[1024,1536]{1,0:T(8,128)(2,1)} %get-tuple-element.9) | copy-start | bytes 9437188
  117.0 39.5 %copy-start.9 = (f32[1536]{0:T(1024)S(1)}, f32[1536]{0:T(1024)}, u32[]{:S(2)}) copy-start(f32[1536]{0:T(1024)} %get-tuple-element.18) | copy-start | bytes 18436
  117.0 39.5 %copy-start.17 = (bf16[1536,1664]{1,0:T(8,128)(2,1)S(1)}, bf16[1536,1664]{1,0:T(8,128)(2,1)}, u32[]{:S(2)}) copy-start(bf16[1536,1664]{1,0:T(8,128)(2,1)} %get-tuple-element.10) | copy-start | bytes 15335428
  162.3 1.0 copy-start.7
  162.3 1.0 copy-start.8
  178.9 0.7 copy-start.14
  178.9 0.7 copy-start.15
  178.9 1.3 copy-start.16
  178.9 1.9 copy-start.11
  179.0 64.6 %copy-start.5 = (f32[2,512,32]{1,2,0:T(8,128)S(1)}, f32[2,512,32]{1,2,0:T(8,128)}, u32[]{:S(2)}) copy-start(f32[2,512,32]{1,2,0:T(8,128)} %param.27) | copy-start | bytes 393220
Sparse Core Ops, SparseCore 0:
  179.1 42.9 reduce-scatter.1

commit v4 on v3

--- a/solution.py
+++ b/solution.py
@@ -404,6 +404,59 @@
     )(vel, par)
 
 
+def feed_kernel(B, x, w1, w2, out, held, inbox, s_sem, r_sem):
+    s, b, c = lax.axis_index("seq"), lax.axis_index("blk"), lax.axis_index("cfg")
+    k = pl.program_id(0)
+    target = (b + 1 + k) % B
+    n = out.shape[0]
+
+    def give(at):
+        return remote(
+            held.at[at], inbox.at[at], s_sem.at[at], r_sem.at[at], (c, s, (b + 1 + at) % B))
+
+    @pl.when(k == 0)
+    def _():
+        greet([(c, s, (b + d) % B) for d in range(1, B)])
+
+    rows = x[pl.ds(pl.multiple_of(target * n, n), n), :]
+    hidden = jax.nn.gelu(dot(rows, w1[...]), approximate=True).astype(jnp.bfloat16)
+    part = dot(hidden, w2[...])
+
+    @pl.when(k < B - 1)
+    def _():
+        held[k] = part.astype(jnp.bfloat16)
+        give(k).start()
+
+    @pl.when(k == B - 1)
+    def _():
+        total = part
+        for at in range(B - 1):
+            give(at).wait()
+            total = total + inbox[at].astype(jnp.float32)
+        out[...] = total
+
+
+def feed_forward(x, w1, w2, B):
+    n, width = x.shape[0] // B, w2.shape[1]
+    dma = pltpu.SemaphoreType.DMA
+    vmem = pl.BlockSpec(memory_space=pltpu.VMEM)
+    return pl.pallas_call(
+        functools.partial(feed_kernel, B),
+        grid=(B,),
+        out_shape=jax.ShapeDtypeStruct((n, width), jnp.float32),
+        in_specs=[vmem] * 3,
+        out_specs=vmem,
+        scratch_shapes=[
+            pltpu.VMEM((B - 1, n, width), jnp.bfloat16),
+            pltpu.VMEM((B - 1, n, width), jnp.bfloat16),
+            dma((B - 1,)), dma((B - 1,)),
+        ],
+        compiler_params=pltpu.CompilerParams(
+            collective_id=4, has_side_effects=True, vmem_limit_bytes=44 * 1024 * 1024
+        ),
+    )(x, w1, w2)
+
+
 def per_device(
     img_hidden, txt_hidden, img_mod, txt_mod, out_mod, w_qkv, w_txt_kv, w_out,
     w_fc1, w_fc2, w_proj, latent, lengths, t_index, stride, guide,
@@ -462,10 +515,7 @@
         jnp.bfloat16
     )
     mlp_in = modulate(resid_one, mod[4:5], mod[3:4])
-    hidden_units = jax.nn.gelu(dot(mlp_in, w_fc1), approximate=True).astype(jnp.bfloat16)
-    mlp_sum = lax.psum_scatter(
-        dot(hidden_units, w_fc2).astype(jnp.bfloat16), "blk", scatter_dimension=0, tiled=True
-    ).astype(jnp.float32)
+    mlp_sum = feed_forward(mlp_in, w_fc1, w_fc2, blk_size)
     resid_own = lax.dynamic_slice_in_dim(resid_one, blk_at * own_rows, own_rows, 0)
     resid_two = (resid_own.astype(jnp.float32) + mod[5:6] * mlp_sum).astype(jnp.bfloat16)
     final_in = modulate(resid_two, fmod[0:1], fmod[1:2])

time: 253 us -> 230 us (0.909)
  Pallas kernels: 141 us -> 185 us
  waiting for transfers between devices: 40 us -> 0.01 us
  between operations: 14.4 us -> 1.05 us
  matrix products: 32.2 us -> 20.7 us
    pallas_call x0 -> x1, Pallas kernels: none -> 42.7 us  [feed_forward(): pl.pallas_call(functools.partial(feed_kernel, B), grid=(B,), out_shape=ja...]
    reduce_scatter x1 -> x0, waiting for transfers between devices: 39.9 us -> none  [per_device(): lax.psum_scatter(dot(hidden_units, w_fc2).astype(jnp.bfloat16), 'blk', sc...]
    dot_general x7 -> x6, matrix products: 30.1 us -> 18.6 us  [dot(): return jnp.dot(a, b, preferred_element_type=jnp.float32)]
  transfers between devices with their start and end apart: 3 -> 2, of which waited for: 1 -> 0; matrix products, arithmetic and copies ran while one was open for 6% -> 6% of each run, Pallas kernels for 14% -> 15%
where the time goes in v4:
time: 230 us; the launch traced here: 229 us
  Pallas kernels  185 us (80%)
  matrix products  20.7 us (9%)
  other arithmetic  14.4 us (6%)
  local copies, waits for them, and re-layouts  6.16 us (3%)
    pallas_call x2, Pallas kernels, attend_piece(): pl.pallas_call(functools.partial(attend_kernel, first, last, S, B, steps)...  74.4 us
    pallas_call x1, Pallas kernels, gather_tokens(): pl.pallas_call(functools.partial(gather_kernel, S, B), out_shape=[jax.Sha...  51.5 us
    pallas_call x1, Pallas kernels, feed_forward(): pl.pallas_call(functools.partial(feed_kernel, B), grid=(B,), out_shape=ja...  42.7 us
    dot_general x6, matrix products, dot(): return jnp.dot(a, b, preferred_element_type=jnp.float32)  18.6 us
    pallas_call x1, Pallas kernels, finish(): pl.pallas_call(functools.partial(tail_kernel, S, B), out_shape=[jax.Shape...  16.5 us
  transfers between devices with their start and end apart: 2, of which 0 were waited for; matrix products, arithmetic and copies ran while one was open for 6% of the time, Pallas kernels for 15%

profile of v4, /device:TPU:0, one launch (start us, length us, event | category | flops | bytes accessed | tf_op | source)
XLA Modules:
  0.0 229.5 jit_solution(12176529110791048861)
XLA Ops:
  0.6 0.0 copy-start
  0.7 1.5 pad.12.txt
  2.1 51.5 %shard_map.167 = (bf16[1024,1536]{1,0:T(8,128)(2,1)}, bf16[192,1536]{1,0:T(8,128)(2,1)}) custom-call(bf16[2,512,384]{2,1,0:T(8,128)(2,1)} %bitcast.59, bf16[2,48,384]{2,1,0:T(8,128)(2,1)} %pad.12.txt), custom_call_target="tpu_custom_call" | custom-call | tf_op jit(solution)/shard_map/pallas_call | solution.py:308
  53.6 0.0 copy-start.1
  53.6 0.0 copy-start.7
  53.6 0.0 copy-start.8
  53.6 2.5 %convert_reduce_fusion = f32[1024]{0:T(1024)S(1)} fusion(bf16[1024,1536]{1,0:T(8,128)(2,1)} %get-tuple-element.9), kind=kLoop, calls=%fused_computation.2 | loop fusion | flops 3144704 | bytes 3149824 | tf_op jit(solution)/shard_map/reduce_sum | solution.py:20
  56.2 0.3 copy-done.1
  56.4 1.0 fusion.4
  57.4 0.0 copy-done.7
  57.4 0.0 copy-done.8
  57.4 0.1 fusion.57
  57.6 0.0 copy-start.10
  57.6 1.5 fusion.7
  59.1 0.5 copy-done.10
  59.6 2.7 %convolution_convert_fusion.1.refs_1_ = bf16[1024,384]{1,0:T(8,128)(2,1)} fusion(bf16[1024,1536]{1,0:T(8,128)(2,1)S(1)} %fusion.7, bf16[3,1536,384]{2,1,0:T(8,128)(2,1)S(1)} %copy-done.10), kind=kOutput, calls=%fused_computation.37 | convolution fusion | flops 1208352768 | bytes 5111808 | tf_op jit(solution)/shard_map/dot_general | solution.py:30
  62.4 1.2 collective-permute-start
  63.6 0.0 copy-done.4
  63.6 2.7 %convolution_convert_fusion.refs_2_ = bf16[1024,384]{1,0:T(8,128)(2,1)} fusion(bf16[1024,1536]{1,0:T(8,128)(2,1)S(1)} %fusion.7, bf16[3,1536,384]{2,1,0:T(8,128)(2,1)S(1)} %copy-done.10), kind=kOutput, calls=%fused_computation.36 | convolution fusion | flops 1208352768 | bytes 5111808 | tf_op jit(solution)/shard_map/dot_general | solution.py:30
  66.3 0.8 collective-permute-start.1
  67.1 0.0 copy-done.9
  67.1 0.0 copy-done.3
  67.1 0.2 convert_reduce_fusion.3
  67.3 0.3 fusion.28
  67.6 0.0 copy-start.6
  67.6 0.0 copy-start.12
  67.7 0.0 copy-start.13
  67.7 0.0 copy-start.14
  67.7 0.4 fusion.31
  68.1 0.0 copy-done.11
  68.1 0.6 fusion.44.refs_6_
  68.7 0.6 fusion.47.refs_7_
  69.3 0.0 copy-done.6
  69.3 0.1 copy.21
  69.4 0.0 copy-done
  69.4 0.6 constant_dynamic-slice_fusion
  70.0 0.7 and_convert_fusion.refs_5_
  70.7 0.0 copy-done.12
  70.7 0.0 copy-done.13
  70.7 0.6 dynamic_slice.30
  71.3 0.0 copy-done.14
  71.3 0.6 dynamic_slice.29
  71.9 1.4 fusion.27.refs_3_
  73.3 1.4 pad_maximum_fusion
  74.6 4.0 %convolution_convert_fusion.2.refs_0_ = bf16[1024,384]{1,0:T(8,128)(2,1)S(1)} fusion(bf16[1024,1536]{1,0:T(8,128)(2,1)} %copy-done.4, bf16[3,1536,384]{2,1,0:T(8,128)(2,1)} %param.21), kind=kOutput, calls=%fused_computation.38 | convolution fusion | flops 1208352768 | bytes 5111808 | tf_op jit(solution)/shard_map/dot_general | solution.py:30
  78.6 34.9 %shard_map.168 = (f32[6,1024,128]{2,1,0:T(8,128)S(1)}, f32[6,1024,128]{2,1,0:T(8,128)S(1)}, bf16[1536,1664]{1,0:T(8,128)(2,1)}) custom-call(bf16[1024,384]{1,0:T(8,128)(2,1)S(1)} %convolution_convert_fusion.2.refs_0_, bf16[1024,384]{1,0:T(8,128)(2,1)} %convolution_convert_fusion.1.refs_1_, bf16[1024,384]{1,0:T(8,128)(2,1)} %convolution_convert_fusion.refs_2_, ...), custom_call_target="tpu_custom_call" | custom-call | flops 3221225472 | bytes 3145728 | tf_op jit(solution)/shard_map/pallas_call | solution.py:226
  113.6 0.0 collective-permute-done.refs_1_
  113.6 0.0 collective-permute-done.1.refs_2_
  113.6 0.0 copy-start.2
  113.6 0.0 slice-start
  113.6 39.5 %shard_map.169 = bf16[1024,1536]{1,0:T(8,128)(2,1)S(1)} custom-call(bf16[1024,384]{1,0:T(8,128)(2,1)S(1)} %convolution_convert_fusion.2.refs_0_, bf16[1024,384]{1,0:T(8,128)(2,1)S(1)} %collective-permute-done.refs_1_, bf16[1024,384]{1,0:T(8,128)(2,1)S(1)} %collective-permute-done.1.refs_2_, f32[6,1024,128]{2,1,0:T(8,128)S(1)} %get-tuple-element.11.refs_3_, ...), custom_call_target="tpu_custom_call" | custom-call | flops 3221225472 | bytes 3145728 | tf_op jit(solution)/shard_map/pallas_call | solution.py:226
  153.1 0.0 slice-start.1
  153.2 8.0 %convert_reduce_fusion.1 = (f32[1024]{0:T(1024)S(1)}, bf16[1024,1536]{1,0:T(8,128)(2,1)S(1)}) fusion(bf16[1024,1536]{1,0:T(8,128)(2,1)S(1)} %shard_map.169, bf16[1536,1664]{1,0:T(8,128)(2,1)} %get-tuple-element.10, f32[1536]{0:T(1024)S(1)} %get-tuple-element.33, bf16[1024,1536]{1,0:T(8,128)(2,1)S(1)} %copy-done.2), kind=kOutput, calls=%fused_computation.4 | convolution fusion | flops 4841274368 | bytes 14166016 | tf_op jit(solution)/shard_map/dot_general | solution.py:30
  161.2 1.0 fusion.8
  162.1 1.7 fusion.11.x
  163.9 42.7 %shard_map.170 = f32[256,1536]{1,0:T(8,128)S(1)} custom-call(bf16[1024,1536]{1,0:T(8,128)(2,1)S(1)} %fusion.11.x, bf16[1536,1536]{1,0:T(8,128)(2,1)S(1)} %bitcast.58, bf16[1536,1536]{1,0:T(8,128)(2,1)} %w2.1), custom_call_target="tpu_custom_call" | custom-call | tf_op jit(solution)/shard_map/pallas_call | solution.py:443
  206.6 0.0 copy-start.5
  206.6 0.3 convert_reduce_fusion.2
  206.9 0.4 fusion.21
  207.3 2.1 convolution_convert_fusion.3
  209.5 0.7 broadcast_in_dim.2.par
  210.1 16.5 %shard_map.171 = (f32[2,32,512]{2,1,0:T(8,128)}, f32[8,128]{1,0:T(8,128)}) custom-call(bf16[2,32,256]{2,1,0:T(8,128)(2,1)} %bitcast.61, f32[2,256]{1,0:T(2,128)} %broadcast_in_dim.2.par), custom_call_target="tpu_custom_call" | custom-call | tf_op jit(solution)/shard_map/pallas_call | solution.py:388
  226.6 1.3 slice_reduce_fusion
  227.9 1.6 bitcast_add_fusion
  (19 shorter events, 0.1 us)
Async XLA Ops:
  0.6 68.8 %copy-start = (s32[1,2]{1,0:T(1,128)S(1)}, s32[1,2]{1,0:T(1,128)}, u32[]{:S(2)}) copy-start(s32[1,2]{1,0:T(1,128)} %param.28) | copy-start | bytes 28
  53.6 2.8 %copy-start.1 = (bf16[1024,1536]{1,0:T(8,128)(2,1)S(1)}, bf16[1024,1536]{1,0:T(8,128)(2,1)}, u32[]{:S(2)}) copy-start(bf16[1024,1536]{1,0:T(8,128)(2,1)} %get-tuple-element.9) | copy-start | bytes 9437188
  53.6 3.8 %copy-start.7 = (f32[1,2,6,1536]{3,1,2,0:T(2,128)S(1)}, f32[1,2,6,1536]{3,1,2,0:T(2,128)}, u32[]{:S(2)}) copy-start(f32[1,2,6,1536]{3,1,2,0:T(2,128)} %param.18) | copy-start | bytes 221188
  53.6 3.8 %copy-start.8 = (f32[1,2,2,1536]{3,2,1,0:T(2,128)S(1)}, f32[1,2,2,1536]{3,2,1,0:T(2,128)}, u32[]{:S(2)}) copy-start(f32[1,2,2,1536]{3,2,1,0:T(2,128)} %param.20) | copy-start | bytes 73732
  57.6 2.0 copy-start.10
  59.6 4.0 %copy-start.4 = (bf16[1024,1536]{1,0:T(8,128)(2,1)}, bf16[1024,1536]{1,0:T(8,128)(2,1)S(1)}, u32[]{:S(2)}) copy-start(bf16[1024,1536]{1,0:T(8,128)(2,1)S(1)} %fusion.7) | copy-start | bytes 9437188
  62.4 4.7 %copy-start.9 = (f32[1,2,2,1536]{3,2,1,0:T(2,128)S(1)}, f32[1,2,2,1536]{3,2,1,0:T(2,128)}, u32[]{:S(2)}) copy-start(f32[1,2,2,1536]{3,2,1,0:T(2,128)} %param.19) | copy-start | bytes 73732
  62.4 4.8 %copy-start.3 = (bf16[192,1536]{1,0:T(8,128)(2,1)S(1)}, bf16[192,1536]{1,0:T(8,128)(2,1)}, u32[]{:S(2)}) copy-start(bf16[192,1536]{1,0:T(8,128)(2,1)} %get-tuple-element.13) | copy-start | bytes 1769476
  62.4 5.7 %copy-start.11 = (bf16[2,1536,384]{2,1,0:T(8,128)(2,1)S(1)}, bf16[2,1536,384]{2,1,0:T(8,128)(2,1)}, u32[]{:S(2)}) copy-start(bf16[2,1536,384]{2,1,0:T(8,128)(2,1)} %param.22) | copy-start | bytes 7077892
  62.4 51.2 %collective-permute-start = (bf16[1024,384]{1,0:T(8,128)(2,1)}, bf16[1024,384]{1,0:T(8,128)(2,1)S(1)}, u32[]{:S(2)}, u32[]{:S(2)}) collective-permute-start(bf16[1024,384]{1,0:T(8,128)(2,1)} %convolution_convert_fusion.1.refs_1_), channel_id=1, source_target_pairs={{0,4},{4,0},{8,12},{12,8},{1,5},{5,1},{9,13},{13,9},{2,6},{6,2},{1... | collective-permute-start | bytes 2359304 | tf_op jit(solution)/shard_map/ppermute | solution.py:490
  66.3 47.3 %collective-permute-start.1 = (bf16[1024,384]{1,0:T(8,128)(2,1)}, bf16[1024,384]{1,0:T(8,128)(2,1)S(1)}, u32[]{:S(2)}, u32[]{:S(2)}) collective-permute-start(bf16[1024,384]{1,0:T(8,128)(2,1)} %convolution_convert_fusion.refs_2_), channel_id=1, source_target_pairs={{0,4},{4,0},{8,12},{12,8},{1,5},{5,1},{9,13},{13,9},{2,6},{6,2},{1... | collective-permute-start | bytes 2359304 | tf_op jit(solution)/shard_map/ppermute | solution.py:490
  67.6 1.6 copy-start.6
  67.6 3.0 %copy-start.12 = (s32[2]{0:T(128)S(1)}, s32[2]{0:T(128)}, u32[]{:S(2)}) copy-start(s32[2]{0:T(128)} %param.29) | copy-start | bytes 28
  67.7 3.0 %copy-start.13 = (s32[2]{0:T(128)S(1)}, s32[2]{0:T(128)}, u32[]{:S(2)}) copy-start(s32[2]{0:T(128)} %param.30) | copy-start | bytes 28
  67.7 3.6 %copy-start.14 = (f32[2]{0:T(128)S(1)}, f32[2]{0:T(128)}, u32[]{:S(2)}) copy-start(f32[2]{0:T(128)} %param.31) | copy-start | bytes 28
  113.6 39.5 %copy-start.2 = (bf16[1024,1536]{1,0:T(8,128)(2,1)S(1)}, bf16[1024,1536]{1,0:T(8,128)(2,1)}, u32[]{:S(2)}) copy-start(bf16[1024,1536]{1,0:T(8,128)(2,1)} %get-tuple-element.9) | copy-start | bytes 9437188
  113.6 50.2 %slice-start = ((s8[4718592]{0:T(1024)(128)(4,1)}), s8[4194304]{0:T(1024)(128)(4,1)S(1)}, s32[]{:S(2)}) async-start(s8[4718592]{0:T(1024)(128)(4,1)} %bitcast.57), calls=%async_computation | async-start | bytes 8388608
  153.1 10.7 %slice-start.1 = ((s8[4718592]{0:T(1024)(128)(4,1)}), s8[524288]{0:T(1024)(128)(4,1)S(1)}, s32[]{:S(2)}) async-start(s8[4718592]{0:T(1024)(128)(4,1)} %bitcast.57), calls=%async_computation.1 | async-start | bytes 1048576
  206.6 21.3 %copy-start.5 = (f32[2,512,32]{1,2,0:T(8,128)S(1)}, f32[2,512,32]{1,2,0:T(8,128)}, u32[]{:S(2)}) copy-start(f32[2,512,32]{1,2,0:T(8,128)} %param.27) | copy-start | bytes 393220
